TPU v7x, 256 devices: a whole 4x4x8 slice. The times are simulated.
256 devices in a mesh: dep: 32 (over y, x, z_hi), hgt: 8 (over z_lo, core).
Axes of the slice: x: 4, y: 4, z: 8 (z_hi: 2, z_lo: 4; z = z_hi * 4 + z_lo), core: 2. Of those that a mesh axis runs over, the one named last changes fastest.
Arguments:
- volume: bfloat16 [64, 64, 64, 512], P('dep', 'hgt'), may hold values from -30 to 30
- qkv_weight: bfloat16 [3, 512, 1536], replicated, may hold values from -2 to 2
- out_weight: bfloat16 [3, 512, 512], replicated, may hold values from -0.25 to 0.25
- norm_gain: float32 [4, 512], replicated, may hold values from 0.1 to 1.9
- up_weight: bfloat16 [512, 2048], replicated, may hold values from -0.25 to 0.25
- down_weight: bfloat16 [2048, 512], replicated, may hold values from -0.125 to 0.125
Outputs:
- result_volume: bfloat16 [64, 64, 64, 512], P('dep', 'hgt')
All inputs are finite; a program needn't handle non-finite values.
Results may differ from a plain program's by a relative error of at most 0.024.
Values may be sent and summed in bfloat16 or wider, within the bound.
No kernel may reach another device: no remote copies, remote signals or barrier semaphores. Data moves between devices by JAX's collectives and lax.ppermute only.
A program may use at most 128 MiB of HBM per device.

v0:
```python
import functools

import jax
import jax.numpy as jnp
from jax import lax
from jax.experimental import pallas as pl
from jax.experimental.pallas import tpu as pltpu
from jax.sharding import Mesh
from jax.sharding import PartitionSpec as P

D = 512
HEADS = 8
HEAD = 64
FF = 2048
LINE = 64
GROUP = 4
ROWS = GROUP * LINE
TOKENS = 1024
EPS = 1e-5
F32 = jnp.float32
BF16 = jnp.bfloat16


def layer_norm(x, gain):
    center = jnp.mean(x, axis=-1, keepdims=True)
    shifted = x - center
    spread = jnp.mean(shifted * shifted, axis=-1, keepdims=True)
    return (shifted * lax.rsqrt(spread + EPS) * gain).astype(BF16)


def attend(x, gain, qkv_ref, out_ref, ones_ref):
    normed = layer_norm(x, gain)
    q = jnp.dot(normed, qkv_ref[:, :D], preferred_element_type=F32)
    q = (q * (HEAD**-0.5)).astype(BF16)
    k = jnp.dot(normed, qkv_ref[:, D : 2 * D], preferred_element_type=F32).astype(BF16)
    v = jnp.dot(normed, qkv_ref[:, 2 * D :], preferred_element_type=F32).astype(BF16)
    wide = 4 * HEAD
    lane_head = lax.broadcasted_iota(jnp.int32, (LINE, wide), 1) // HEAD
    low = lax.broadcasted_iota(jnp.int32, (LINE, 128), 1) < HEAD
    zero = jnp.zeros((LINE, wide), BF16)
    halves = []
    for g in range(2):
        cols = slice(g * wide, (g + 1) * wide)
        exps = []
        mixed = []
        for line in range(GROUP):
            rows = slice(line * LINE, (line + 1) * LINE)
            kk, vv = k[rows, cols], v[rows, cols]
            k_diag = jnp.concatenate(
                [jnp.where(lane_head == h, kk, zero) for h in range(4)], axis=0
            )
            v_diag = jnp.concatenate(
                [jnp.where(lane_head == h, vv, zero) for h in range(4)], axis=0
            )
            scores = lax.dot_general(
                q[rows, cols], k_diag, (((1,), (1,)), ((), ())), preferred_element_type=F32
            )
            parts = []
            for half in range(2):
                s = scores[:, half * 128 : (half + 1) * 128]
                top_low = jnp.max(jnp.where(low, s, -jnp.inf), axis=-1, keepdims=True)
                top_high = jnp.max(jnp.where(low, -jnp.inf, s), axis=-1, keepdims=True)
                parts.append(jnp.exp(s - jnp.where(low, top_low, top_high)).astype(BF16))
            e = jnp.concatenate(parts, axis=1)
            exps.append(e)
            mixed.append(jnp.dot(e, v_diag, preferred_element_type=F32))
        sums = jnp.dot(
            jnp.concatenate(exps, axis=0), ones_ref[...], preferred_element_type=F32
        )
        halves.append((jnp.concatenate(mixed, axis=0) / sums).astype(BF16))
    attended = jnp.concatenate(halves, axis=1)
    return x + jnp.dot(attended, out_ref[...], preferred_element_type=F32)


def width_kernel(x_ref, gain_ref, qkv_ref, out_w_ref, ones_ref, y_ref):
    x = x_ref[...].reshape(ROWS, D).astype(F32)
    y = attend(x, gain_ref[0:1, :], qkv_ref, out_w_ref, ones_ref)
    for z in range(8):
        pieces = [y[h * LINE + 8 * z : h * LINE + 8 * z + 8, :] for h in range(GROUP)]
        y_ref[z, 0] = jnp.concatenate(pieces, axis=0).astype(BF16)


def spread(x_ref, xs):
    for c in range(4):
        xs[c] = x_ref[:, c * 128 : (c + 1) * 128].astype(F32)


def gather(ys, y_ref):
    for c in range(4):
        y_ref[:, c * 128 : (c + 1) * 128] = ys[c].astype(BF16)


def take(xs, start, count, stride):
    return jnp.concatenate([xs[c, pl.ds(start, count, stride=stride), :] for c in range(4)], axis=1)


def put(ys, start, count, stride, value):
    for c in range(4):
        ys[c, pl.ds(start, count, stride=stride), :] = value[:, c * 128 : (c + 1) * 128]


def height_kernel(x_ref, gain_ref, qkv_ref, out_w_ref, ones_ref, y_ref, xs, ys):
    spread(x_ref, xs)

    def step(i, carry):
        zh, wsub = i // 2, i % 2
        x = jnp.concatenate(
            [take(xs, zh * 512 + wsub * 4 + w4, LINE, 8) for w4 in range(4)], axis=0
        )
        y = attend(x, gain_ref[1:2, :], qkv_ref, out_w_ref, ones_ref)
        for w4 in range(4):
            for zl in range(4):
                for c in range(2):
                    at = w4 * LINE + (zl * 2 + c) * 8
                    start = wsub * 64 + c * 32 + zl * 8 + zh * 4 + w4
                    put(ys, start, 8, 128, y[at : at + 8, :])
        return carry

    lax.fori_loop(0, 4, step, 0)
    gather(ys, y_ref)


def depth_kernel(x_ref, gain_ref, qkv_ref, out_w_ref, ones_ref, up_ref, down_ref, y_ref, xs, ys):
    spread(x_ref, xs)

    def step(zl, carry):
        x = jnp.concatenate(
            [
                take(xs, d0 * 32 + zl * 8 + zh * 4 + w4, 16, 64)
                for w4 in range(4)
                for zh in range(2)
                for d0 in range(2)
            ],
            axis=0,
        )
        x = attend(x, gain_ref[2:3, :], qkv_ref, out_w_ref, ones_ref)
        x = x.astype(BF16).astype(F32)
        normed = layer_norm(x, gain_ref[3:4, :])
        total = x
        for part in range(4):
            cols = slice(part * 512, (part + 1) * 512)
            hidden = jnp.dot(normed, up_ref[:, cols], preferred_element_type=F32)
            hidden = jax.nn.gelu(hidden).astype(BF16)
            total = total + jnp.dot(hidden, down_ref[cols, :], preferred_element_type=F32)
        for w4 in range(4):
            for zh in range(2):
                for d0 in range(2):
                    at = w4 * LINE + (zh * 2 + d0) * 16
                    start = zh * 32 + zl * 8 + d0 * 4 + w4
                    put(ys, start, 16, 64, total[at : at + 16, :])
        return carry

    lax.fori_loop(0, 4, step, 0)
    gather(ys, y_ref)


def place_kernel(x_ref, y_ref):
    low = lax.broadcasted_iota(jnp.int32, (LINE, D), 0) % 8 < 4
    first = x_ref[0, 0].astype(F32)
    second = x_ref[0, 1].astype(F32)
    y_ref[0, 0] = jnp.where(low, first, pltpu.roll(second, 4, 0)).astype(BF16)
    y_ref[1, 0] = jnp.where(low, pltpu.roll(first, LINE - 4, 0), second).astype(BF16)


PARAMS = pltpu.CompilerParams(vmem_limit_bytes=40 * 1024 * 1024)


def ones_block():
    head = jnp.arange(4 * HEAD) // HEAD
    return (head[:, None] == head[None, :]).astype(BF16)


def weight_specs(layer):
    return [
        pl.BlockSpec((4, D), lambda *i: (0, 0)),
        pl.BlockSpec((None, D, 3 * D), lambda *i: (layer, 0, 0)),
        pl.BlockSpec((None, D, D), lambda *i: (layer, 0, 0)),
        pl.BlockSpec((4 * HEAD, 4 * HEAD), lambda *i: (0, 0)),
    ]


def whole(*shape):
    return pl.BlockSpec(shape, lambda *i: (0,) * len(shape))


def body(volume, qkv_weight, out_weight, norm_gain, up_weight, down_weight):
    ones = ones_block()
    weights = (norm_gain, qkv_weight, out_weight, ones)
    sent = pl.pallas_call(
        width_kernel,
        grid=(4,),
        in_specs=[pl.BlockSpec((1, 4, LINE, D), lambda i: (i // 2, i % 2, 0, 0))] + weight_specs(0),
        out_specs=pl.BlockSpec((8, 1, 32, D), lambda i: (0, i // 2, i % 2, 0)),
        out_shape=jax.ShapeDtypeStruct((8, 2, 64, D), BF16),
        compiler_params=PARAMS,
        name="width",
    )(volume, *weights)
    sent = sent.reshape(16, 64, D)
    held = lax.all_to_all(sent, ("zh", "zl", "c"), split_axis=0, concat_axis=0, tiled=True)
    scratch = [pltpu.VMEM((4, TOKENS, 128), F32), pltpu.VMEM((4, TOKENS, 128), F32)]
    sent = pl.pallas_call(
        height_kernel,
        grid=(1,),
        in_specs=[whole(TOKENS, D)] + weight_specs(1),
        out_specs=whole(TOKENS, D),
        out_shape=jax.ShapeDtypeStruct((TOKENS, D), BF16),
        scratch_shapes=scratch,
        compiler_params=PARAMS,
        name="height",
    )(held.reshape(TOKENS, D), *weights)
    sent = sent.reshape(32, 32, D)
    held = lax.all_to_all(sent, ("y", "x", "c"), split_axis=0, concat_axis=0, tiled=True)
    sent = pl.pallas_call(
        depth_kernel,
        grid=(1,),
        in_specs=[whole(TOKENS, D)] + weight_specs(2) + [whole(D, FF), whole(FF, D)],
        out_specs=whole(TOKENS, D),
        out_shape=jax.ShapeDtypeStruct((TOKENS, D), BF16),
        scratch_shapes=scratch,
        compiler_params=PARAMS,
        name="depth",
    )(held.reshape(TOKENS, D), *weights, up_weight, down_weight)
    sent = sent.reshape(128, 8, D)
    held = lax.all_to_all(sent, ("y", "x", "zh", "zl"), split_axis=0, concat_axis=0, tiled=True)
    return pl.pallas_call(
        place_kernel,
        grid=(8,),
        in_specs=[pl.BlockSpec((1, 2, LINE, D), lambda i: (i, 0, 0, 0))],
        out_specs=pl.BlockSpec((2, 1, LINE, D), lambda i: (0, i, 0, 0)),
        out_shape=jax.ShapeDtypeStruct((2, 8, LINE, D), BF16),
        compiler_params=PARAMS,
        name="place",
    )(held.reshape(8, 2, LINE, D))


def solution(mesh):
    fine = Mesh(mesh.devices.reshape(4, 4, 2, 4, 2), ("y", "x", "zh", "zl", "c"))
    return jax.shard_map(
        body,
        mesh=fine,
        in_specs=(P(("y", "x", "zh"), ("zl", "c"), None, None), P(), P(), P(), P(), P()),
        out_specs=P(("y", "x", "zh"), ("zl", "c"), None, None),
        check_vma=False,
    )
```

profile of v0, /device:TPU:1, one launch (start us, length us, event | category | flops | bytes accessed | tf_op | source)
XLA Modules:
  0.0 153.6 jit_solution(17473830288905627980)
XLA Ops:
  0.0 0.1 compare_convert_fusion.ones_ref
  0.1 0.0 copy-start
  0.1 2.3 %copy-done = bf16[3,512,1536]{2,1,0:T(8,128)(2,1)S(1)} copy-done((bf16[3,512,1536]{2,1,0:T(8,128)(2,1)S(1)}, bf16[3,512,1536]{2,1,0:T(8,128)(2,1)}, u32[]{:S(2)}) %copy-start) | copy-done | bytes 4718616
  2.5 0.0 copy-start.2
  2.5 1.4 copy-done.2
  3.9 0.0 copy-start.6
  3.9 1.2 copy-done.6
  5.1 0.0 copy-start.7
  5.1 0.7 copy-done.7
  5.8 0.0 copy-start.1
  5.8 10.3 %width.1 = bf16[8,2,64,512]{3,2,1,0:T(8,128)(2,1)S(1)} custom-call(bf16[2,8,64,512]{3,2,1,0:T(8,128)(2,1)S(1)} %copy-done.6, f32[4,512]{1,0:T(4,128)S(1)} %copy-done.7, bf16[3,512,1536]{2,1,0:T(8,128)(2,1)S(1)} %copy-done, bf16[3,512,512]{2,1,0:T(8,128)(2,1)S(1)} %copy-done.2, bf16[256,256]{1,0:T(8,128)(2,1)S(1)} %compare_convert_fusion.ones_ref), custom_call_target="tpu_custom_call" | custom-call | tf_op jit(solution)/shard_map/width/pallas_call | solution.py:189
  16.1 0.0 copy-start.3
  16.1 0.0 copy-start.8
  16.1 38.5 %all_to_all.15 = bf16[16,64,512]{2,1,0:T(8,128)(2,1)S(1)} all-to-all(bf16[16,64,512]{2,1,0:T(8,128)(2,1)S(1)} %bitcast.8), channel_id=1, replica_groups=mesh['y'=4,'x'=4,'zh'=2,'zl'=4,'c'=2] {'zh','zl','c'}, dimensions={0} | all-to-all | bytes 2097152 | tf_op jit(solution)/shard_map/all_to_all | solution.py:199
  54.6 0.0 copy-done.1
  54.6 0.0 copy-done.3
  54.6 0.0 copy-done.8
  54.6 0.0 copy-start.5
  54.6 12.3 %height.1 = bf16[1024,512]{1,0:T(8,128)(2,1)S(1)} custom-call(bf16[1024,512]{1,0:T(8,128)(2,1)S(1)} %bitcast.6, f32[4,512]{1,0:T(4,128)S(1)} %copy-done.8, bf16[3,512,1536]{2,1,0:T(8,128)(2,1)S(1)} %copy-done.1, bf16[3,512,512]{2,1,0:T(8,128)(2,1)S(1)} %copy-done.3, bf16[256,256]{1,0:T(8,128)(2,1)S(1)} %compare_convert_fusion.ones_ref), custom_call_target="tpu_custom_call" | custom-call | tf_op jit(solution)/shard_map/height/pallas_call | solution.py:201
  66.9 0.0 copy-start.4
  67.0 24.3 %all_to_all.16 = bf16[32,32,512]{2,1,0:T(8,128)(2,1)S(1)} all-to-all(bf16[32,32,512]{2,1,0:T(8,128)(2,1)S(1)} %bitcast.7), channel_id=1, replica_groups=mesh['y'=4,'x'=4,'zh'=2,'zl'=4,'c'=2] {'y','x','c'}, dimensions={0} | all-to-all | bytes 2097152 | tf_op jit(solution)/shard_map/all_to_all | solution.py:212
  91.3 0.0 copy-done.5
  91.3 0.0 copy-done.4
  91.3 22.0 %depth.1 = bf16[1024,512]{1,0:T(8,128)(2,1)S(1)} custom-call(bf16[1024,512]{1,0:T(8,128)(2,1)S(1)} %bitcast.10, f32[4,512]{1,0:T(4,128)S(1)} %copy-done.8, bf16[3,512,1536]{2,1,0:T(8,128)(2,1)S(1)} %copy-done.1, bf16[3,512,512]{2,1,0:T(8,128)(2,1)S(1)} %copy-done.3, bf16[256,256]{1,0:T(8,128)(2,1)S(1)} %compare_convert_fusion.ones_ref, ...), custom_call_target="tpu_custom_call" | custom-call | tf_op jit(solution)/shard_map/depth/pallas_call | solution.py:213
  113.3 37.4 %all_to_all.17 = bf16[128,8,512]{2,1,0:T(8,128)(2,1)S(1)} all-to-all(bf16[128,8,512]{2,1,0:T(8,128)(2,1)S(1)} %bitcast.11), channel_id=1, replica_groups=mesh['y'=4,'x'=4,'zh'=2,'zl'=4,'c'=2] {'y','x','zh','zl'}, dimensions={0} | all-to-all | bytes 2097152 | tf_op jit(solution)/shard_map/all_to_all | solution.py:224
  150.7 2.9 %place.1 = bf16[2,8,64,512]{3,2,1,0:T(8,128)(2,1)} custom-call(bf16[8,2,64,512]{3,2,1,0:T(8,128)(2,1)S(1)} %bitcast.9), custom_call_target="tpu_custom_call" | custom-call | tf_op jit(solution)/shard_map/place/pallas_call | solution.py:225
  (1 shorter events, 0.0 us)
Async XLA Ops:
  0.1 2.3 %copy-start = (bf16[3,512,1536]{2,1,0:T(8,128)(2,1)S(1)}, bf16[3,512,1536]{2,1,0:T(8,128)(2,1)}, u32[]{:S(2)}) copy-start(bf16[3,512,1536]{2,1,0:T(8,128)(2,1)} %qkv_ref.5) | copy-start | bytes 14155780
  2.5 1.4 copy-start.2
  3.9 1.2 copy-start.6
  5.1 0.7 copy-start.7
  5.8 48.8 %copy-start.1 = (bf16[3,512,1536]{2,1,0:T(8,128)(2,1)S(1)}, bf16[3,512,1536]{2,1,0:T(8,128)(2,1)}, u32[]{:S(2)}) copy-start(bf16[3,512,1536]{2,1,0:T(8,128)(2,1)} %qkv_ref.5) | copy-start | bytes 14155780
  16.1 38.5 %copy-start.3 = (bf16[3,512,512]{2,1,0:T(8,128)(2,1)S(1)}, bf16[3,512,512]{2,1,0:T(8,128)(2,1)}, u32[]{:S(2)}) copy-start(bf16[3,512,512]{2,1,0:T(8,128)(2,1)} %out_w_ref.5) | copy-start | bytes 4718596
  16.1 38.5 %copy-start.8 = (f32[4,512]{1,0:T(4,128)S(1)}, f32[4,512]{1,0:T(4,128)}, u32[]{:S(2)}) copy-start(f32[4,512]{1,0:T(4,128)} %gain_ref.5) | copy-start | bytes 24580
  54.6 36.7 %copy-start.5 = (bf16[2048,512]{1,0:T(8,128)(2,1)S(1)}, bf16[2048,512]{1,0:T(8,128)(2,1)}, u32[]{:S(2)}) copy-start(bf16[2048,512]{1,0:T(8,128)(2,1)} %down_ref.1) | copy-start | bytes 6291460
  66.9 24.3 %copy-start.4 = (bf16[512,2048]{1,0:T(8,128)(2,1)S(1)}, bf16[512,2048]{1,0:T(8,128)(2,1)}, u32[]{:S(2)}) copy-start(bf16[512,2048]{1,0:T(8,128)(2,1)} %up_ref.1) | copy-start | bytes 6291460
where the time goes:
time: 154 us
  blocking collectives  100 us (65%)
  Pallas kernels  47.6 us (31%)
  local copies, waits for them, and re-layouts  5.69 us (4%)
    all_to_all x1, blocking collectives, body(): lax.all_to_all(sent, ('zh', 'zl', 'c'), split_axis=0, concat_axis=0, tile...  38.5 us
    all_to_all x1, blocking collectives, body(): lax.all_to_all(sent, ('y', 'x', 'zh', 'zl'), split_axis=0, concat_axis=0,...  37.4 us
    all_to_all x1, blocking collectives, body(): lax.all_to_all(sent, ('y', 'x', 'c'), split_axis=0, concat_axis=0, tiled=...  24.3 us
    pallas_call x1, Pallas kernels, body(): pl.pallas_call(depth_kernel, grid=(1,), in_specs=[whole(TOKENS, D)] + wei...  22 us
    pallas_call x1, Pallas kernels, body(): pl.pallas_call(height_kernel, grid=(1,), in_specs=[whole(TOKENS, D)] + we...  12.3 us
    pallas_call x1, Pallas kernels, body(): pl.pallas_call(width_kernel, grid=(4,), in_specs=[pl.BlockSpec((1, 4, LIN...  10.3 us
    unnamed x18, local copies, waits for them, and re-layouts  5.69 us

commit v1 on v0

v1 whole, which is shorter than its diff:
```python
import functools

import jax
import jax.numpy as jnp
from jax import lax
from jax.experimental import pallas as pl
from jax.experimental.pallas import tpu as pltpu
from jax.sharding import Mesh
from jax.sharding import PartitionSpec as P

D = 512
HEADS = 8
HEAD = 64
FF = 2048
LINE = 64
TOKENS = 1024
EPS = 1e-5
F32 = jnp.float32
BF16 = jnp.bfloat16


def layer_norm(x, gain):
    center = jnp.mean(x, axis=-1, keepdims=True)
    shifted = x - center
    spread = jnp.mean(shifted * shifted, axis=-1, keepdims=True)
    return (shifted * lax.rsqrt(spread + EPS) * gain).astype(BF16)


def dot(a, b):
    return jnp.dot(a, b, preferred_element_type=F32)


def softmax_top(scores, low):
    parts = []
    for half in range(2):
        s = scores[:, half * 128 : (half + 1) * 128]
        top_low = jnp.max(jnp.where(low, s, -jnp.inf), axis=-1, keepdims=True)
        top_high = jnp.max(jnp.where(low, -jnp.inf, s), axis=-1, keepdims=True)
        parts.append(jnp.exp(s - jnp.where(low, top_low, top_high)).astype(BF16))
    return jnp.concatenate(parts, axis=1)


def attend(x, gain, qkv_ref, out_ref, ones_ref):
    n = x.shape[0] // LINE
    normed = layer_norm(x, gain)
    q = (dot(normed, qkv_ref[:, :D]) * (HEAD**-0.5)).astype(BF16)
    k = dot(normed, qkv_ref[:, D : 2 * D]).astype(BF16).T
    v = dot(normed, qkv_ref[:, 2 * D :]).astype(BF16)
    low_row = lax.broadcasted_iota(jnp.int32, (1, 128), 1) < HEAD
    even = jnp.where(low_row, 1.0, 0.0).astype(BF16)
    odd = jnp.where(low_row, 0.0, 1.0).astype(BF16)
    low = lax.broadcasted_iota(jnp.int32, (LINE, 128), 1) < HEAD
    wide_low = lax.broadcasted_iota(jnp.int32, (LINE, 256), 1) % 128 < HEAD
    zero = jnp.zeros((128, 128), BF16)

    def diagonal(a, b):
        return jnp.concatenate(
            [jnp.concatenate([a, zero], axis=1), jnp.concatenate([zero, b], axis=1)], axis=0
        )

    exps = [[], []]
    mixed = [[], []]
    for pair in range(n // 2):
        at = 128 * pair
        a, b = slice(at, at + LINE), slice(at + LINE, at + 128)
        cells = []
        for p in range(4):
            c = slice(128 * p, 128 * p + 128)
            top = k[128 * p : 128 * p + 64, at : at + 128]
            bottom = k[128 * p + 64 : 128 * p + 128, at : at + 128]
            cells.append(
                (
                    (
                        q[a, c] * even + q[b, c] * odd,
                        jnp.concatenate([top * even, bottom * odd], axis=0),
                        jnp.concatenate([v[a, c] * even, v[b, c] * odd], axis=0),
                    ),
                    (
                        q[b, c] * even + q[a, c] * odd,
                        jnp.concatenate([top * odd, bottom * even], axis=0),
                        jnp.concatenate([v[a, c] * odd, v[b, c] * even], axis=0),
                    ),
                )
            )
        for g in range(2):
            for i in range(2):
                first, second = cells[2 * g][i], cells[2 * g + 1][i]
                scores = dot(
                    jnp.concatenate([first[0], second[0]], axis=1), diagonal(first[1], second[1])
                )
                e = softmax_top(scores, low)
                exps[i].append(e)
                mixed[i].append(dot(e, diagonal(first[2], second[2])))
    sums = [dot(jnp.concatenate(exps[i], axis=0), ones_ref[i]) for i in range(2)]
    rows = []
    for pair in range(n // 2):
        of_a, of_b = [], []
        for g in range(2):
            at = 2 * pair + g
            r = [mixed[i][at] / sums[i][at * LINE : (at + 1) * LINE] for i in range(2)]
            of_a.append(jnp.where(wide_low, r[0], r[1]).astype(BF16))
            of_b.append(jnp.where(wide_low, r[1], r[0]).astype(BF16))
        rows += [jnp.concatenate(of_a, axis=1), jnp.concatenate(of_b, axis=1)]
    return x + dot(jnp.concatenate(rows, axis=0), out_ref[...])


def width_kernel(x_ref, gain_ref, qkv_ref, out_w_ref, ones_ref, y_ref):
    x = x_ref[...].reshape(TOKENS, D).astype(F32)
    y = attend(x, gain_ref[0:1, :], qkv_ref, out_w_ref, ones_ref)
    for d in range(2):
        for z in range(8):
            pieces = [y[(d * 8 + h) * LINE + 8 * z :][:8] for h in range(8)]
            y_ref[z, d] = jnp.concatenate(pieces, axis=0).astype(BF16)


def spread(x_ref, xs):
    for c in range(4):
        xs[c] = x_ref[:, c * 128 : (c + 1) * 128].astype(F32)


def gather(ys, y_ref):
    for c in range(4):
        y_ref[:, c * 128 : (c + 1) * 128] = ys[c].astype(BF16)


def take(xs, start, count, stride):
    return jnp.concatenate([xs[c, pl.ds(start, count, stride=stride), :] for c in range(4)], axis=1)


def put(ys, start, count, stride, value):
    for c in range(4):
        ys[c, pl.ds(start, count, stride=stride), :] = value[:, c * 128 : (c + 1) * 128]


def height_kernel(x_ref, gain_ref, qkv_ref, out_w_ref, ones_ref, y_ref, xs, ys):
    spread(x_ref, xs)
    lines = [(zh, w) for zh in range(2) for w in range(8)]
    x = jnp.concatenate([take(xs, zh * 512 + w, LINE, 8) for zh, w in lines], axis=0)
    y = attend(x, gain_ref[1:2, :], qkv_ref, out_w_ref, ones_ref)
    for n, (zh, w) in enumerate(lines):
        for zl in range(4):
            for c in range(2):
                start = (w // 4) * 64 + c * 32 + zl * 8 + zh * 4 + w % 4
                put(ys, start, 8, 128, y[n * LINE + (zl * 2 + c) * 8 :][:8])
    gather(ys, y_ref)


def depth_kernel(x_ref, gain_ref, qkv_ref, out_w_ref, ones_ref, up_ref, down_ref, y_ref, xs, ys):
    spread(x_ref, xs)
    lines = [(zl, w4) for zl in range(4) for w4 in range(4)]
    quarters = [(zh, d0) for zh in range(2) for d0 in range(2)]
    x = jnp.concatenate(
        [
            take(xs, d0 * 32 + zl * 8 + zh * 4 + w4, 16, 64)
            for zl, w4 in lines
            for zh, d0 in quarters
        ],
        axis=0,
    )
    x = attend(x, gain_ref[2:3, :], qkv_ref, out_w_ref, ones_ref)
    x = x.astype(BF16).astype(F32)
    normed = layer_norm(x, gain_ref[3:4, :])
    total = x
    for part in range(4):
        cols = slice(part * 512, (part + 1) * 512)
        hidden = jax.nn.gelu(dot(normed, up_ref[:, cols])).astype(BF16)
        total = total + dot(hidden, down_ref[cols, :])
    for n, (zl, w4) in enumerate(lines):
        for m, (zh, d0) in enumerate(quarters):
            put(ys, zh * 32 + zl * 8 + d0 * 4 + w4, 16, 64, total[n * LINE + m * 16 :][:16])
    gather(ys, y_ref)


def place_kernel(x_ref, y_ref):
    low = lax.broadcasted_iota(jnp.int32, (LINE, D), 0) % 8 < 4
    for hs in range(8):
        first = x_ref[hs, 0].astype(F32)
        second = x_ref[hs, 1].astype(F32)
        y_ref[0, hs] = jnp.where(low, first, pltpu.roll(second, 4, 0)).astype(BF16)
        y_ref[1, hs] = jnp.where(low, pltpu.roll(first, LINE - 4, 0), second).astype(BF16)


PARAMS = pltpu.CompilerParams(vmem_limit_bytes=40 * 1024 * 1024)


def ones_block():
    head = jnp.arange(4 * HEAD) // HEAD
    straight = head[:, None] == head[None, :]
    crossed = head[:, None] == head[None, :] + 1 - 2 * (head[None, :] % 2)
    return jnp.stack([straight, crossed]).astype(BF16)


def weight_specs(layer):
    return [
        pl.BlockSpec((4, D), lambda *i: (0, 0)),
        pl.BlockSpec((None, D, 3 * D), lambda *i: (layer, 0, 0)),
        pl.BlockSpec((None, D, D), lambda *i: (layer, 0, 0)),
        pl.BlockSpec((2, 4 * HEAD, 4 * HEAD), lambda *i: (0, 0, 0)),
    ]


def whole(*shape):
    return pl.BlockSpec(shape, lambda *i: (0,) * len(shape))


def body(volume, qkv_weight, out_weight, norm_gain, up_weight, down_weight):
    ones = ones_block()
    weights = (norm_gain, qkv_weight, out_weight, ones)
    sent = pl.pallas_call(
        width_kernel,
        grid=(1,),
        in_specs=[whole(2, 8, LINE, D)] + weight_specs(0),
        out_specs=whole(8, 2, 64, D),
        out_shape=jax.ShapeDtypeStruct((8, 2, 64, D), BF16),
        compiler_params=PARAMS,
        name="width",
    )(volume, *weights)
    sent = sent.reshape(16, 64, D)
    held = lax.all_to_all(sent, ("zh", "zl", "c"), split_axis=0, concat_axis=0, tiled=True)
    scratch = [pltpu.VMEM((4, TOKENS, 128), F32), pltpu.VMEM((4, TOKENS, 128), F32)]
    sent = pl.pallas_call(
        height_kernel,
        grid=(1,),
        in_specs=[whole(TOKENS, D)] + weight_specs(1),
        out_specs=whole(TOKENS, D),
        out_shape=jax.ShapeDtypeStruct((TOKENS, D), BF16),
        scratch_shapes=scratch,
        compiler_params=PARAMS,
        name="height",
    )(held.reshape(TOKENS, D), *weights)
    sent = sent.reshape(32, 32, D)
    held = lax.all_to_all(sent, ("y", "x", "c"), split_axis=0, concat_axis=0, tiled=True)
    sent = pl.pallas_call(
        depth_kernel,
        grid=(1,),
        in_specs=[whole(TOKENS, D)] + weight_specs(2) + [whole(D, FF), whole(FF, D)],
        out_specs=whole(TOKENS, D),
        out_shape=jax.ShapeDtypeStruct((TOKENS, D), BF16),
        scratch_shapes=scratch,
        compiler_params=PARAMS,
        name="depth",
    )(held.reshape(TOKENS, D), *weights, up_weight, down_weight)
    sent = sent.reshape(128, 8, D)
    held = lax.all_to_all(sent, ("y", "x", "zh", "zl"), split_axis=0, concat_axis=0, tiled=True)
    return pl.pallas_call(
        place_kernel,
        grid=(1,),
        in_specs=[whole(8, 2, LINE, D)],
        out_specs=whole(2, 8, LINE, D),
        out_shape=jax.ShapeDtypeStruct((2, 8, LINE, D), BF16),
        compiler_params=PARAMS,
        name="place",
    )(held.reshape(8, 2, LINE, D))


def solution(mesh):
    fine = Mesh(mesh.devices.reshape(4, 4, 2, 4, 2), ("y", "x", "zh", "zl", "c"))
    return jax.shard_map(
        body,
        mesh=fine,
        in_specs=(P(("y", "x", "zh"), ("zl", "c"), None, None), P(), P(), P(), P(), P()),
        out_specs=P(("y", "x", "zh"), ("zl", "c"), None, None),
        check_vma=False,
    )
```

time: 154 us -> 133 us (0.86)
  Pallas kernels: 47.6 us -> 26.6 us
    pallas_call x1, Pallas kernels: 22 us -> 14.3 us  [body(): pl.pallas_call(depth_kernel, grid=(1,), in_specs=[whole(TOKENS, D)] + wei...]
    pallas_call x2, Pallas kernels: 13.2 us -> 5.88 us  [the longest x1 4.57 us: body(): pl.pallas_call(width_kernel, grid=(1,), in_specs=[whole(2, 8, LINE, D)] +...]
    pallas_call x1, Pallas kernels: 12.3 us -> 6.41 us  [body(): pl.pallas_call(height_kernel, grid=(1,), in_specs=[whole(TOKENS, D)] + we...]
where the time goes in v1:
time: 133 us
  blocking collectives  100 us (75%)
  Pallas kernels  26.6 us (20%)
  local copies, waits for them, and re-layouts  5.69 us (4%)
    all_to_all x1, blocking collectives, body(): lax.all_to_all(sent, ('zh', 'zl', 'c'), split_axis=0, concat_axis=0, tile...  38.5 us
    all_to_all x1, blocking collectives, body(): lax.all_to_all(sent, ('y', 'x', 'zh', 'zl'), split_axis=0, concat_axis=0,...  37.4 us
    all_to_all x1, blocking collectives, body(): lax.all_to_all(sent, ('y', 'x', 'c'), split_axis=0, concat_axis=0, tiled=...  24.3 us
    pallas_call x1, Pallas kernels, body(): pl.pallas_call(depth_kernel, grid=(1,), in_specs=[whole(TOKENS, D)] + wei...  14.3 us
    pallas_call x1, Pallas kernels, body(): pl.pallas_call(height_kernel, grid=(1,), in_specs=[whole(TOKENS, D)] + we...  6.41 us
    unnamed x18, local copies, waits for them, and re-layouts  5.69 us
    pallas_call x1, Pallas kernels, body(): pl.pallas_call(width_kernel, grid=(1,), in_specs=[whole(2, 8, LINE, D)] +...  4.57 us

profile of v1, /device:TPU:1, one launch (start us, length us, event | category | flops | bytes accessed | tf_op | source)
XLA Modules:
  0.0 132.7 jit_solution(1040766318661825778)
XLA Ops:
  0.0 0.1 broadcast_compare_fusion.1
  0.2 0.0 copy-start
  0.2 2.3 %copy-done = bf16[3,512,1536]{2,1,0:T(8,128)(2,1)S(1)} copy-done((bf16[3,512,1536]{2,1,0:T(8,128)(2,1)S(1)}, bf16[3,512,1536]{2,1,0:T(8,128)(2,1)}, u32[]{:S(2)}) %copy-start) | copy-done | bytes 4718616
  2.5 0.0 copy-start.2
  2.5 1.4 %copy-done.2 = bf16[3,512,512]{2,1,0:T(8,128)(2,1)S(1)} copy-done((bf16[3,512,512]{2,1,0:T(8,128)(2,1)S(1)}, bf16[3,512,512]{2,1,0:T(8,128)(2,1)}, u32[]{:S(2)}) %copy-start.2) | copy-done | bytes 1572888
  3.9 0.0 copy-start.6
  3.9 1.2 copy-done.6
  5.2 0.0 copy-start.7
  5.2 0.7 copy-done.7
  5.9 0.0 copy-start.1
  5.9 4.6 %width.1 = bf16[8,2,64,512]{3,2,1,0:T(8,128)(2,1)S(1)} custom-call(bf16[2,8,64,512]{3,2,1,0:T(8,128)(2,1)S(1)} %copy-done.6, f32[4,512]{1,0:T(4,128)S(1)} %copy-done.7, bf16[3,512,1536]{2,1,0:T(8,128)(2,1)S(1)} %copy-done, bf16[3,512,512]{2,1,0:T(8,128)(2,1)S(1)} %copy-done.2, bf16[2,256,256]{2,1,0:T(8,128)(2,1)S(1)} %add_convert_fusion.ones_ref), custom_call_target="tpu_custom_call" | custom-call | tf_op jit(solution)/shard_map/width/pallas_call | solution.py:209
  10.4 0.0 copy-start.3
  10.5 0.0 copy-start.8
  10.5 38.5 %all_to_all.15 = bf16[16,64,512]{2,1,0:T(8,128)(2,1)S(1)} all-to-all(bf16[16,64,512]{2,1,0:T(8,128)(2,1)S(1)} %bitcast.8), channel_id=1, replica_groups=mesh['y'=4,'x'=4,'zh'=2,'zl'=4,'c'=2] {'zh','zl','c'}, dimensions={0} | all-to-all | bytes 2097152 | tf_op jit(solution)/shard_map/all_to_all | solution.py:219
  48.9 0.0 copy-done.1
  49.0 0.0 copy-done.3
  49.0 0.0 copy-done.8
  49.0 0.0 copy-start.5
  49.0 6.4 %height.1 = bf16[1024,512]{1,0:T(8,128)(2,1)S(1)} custom-call(bf16[1024,512]{1,0:T(8,128)(2,1)S(1)} %bitcast.6, f32[4,512]{1,0:T(4,128)S(1)} %copy-done.8, bf16[3,512,1536]{2,1,0:T(8,128)(2,1)S(1)} %copy-done.1, bf16[3,512,512]{2,1,0:T(8,128)(2,1)S(1)} %copy-done.3, bf16[2,256,256]{2,1,0:T(8,128)(2,1)S(1)} %add_convert_fusion.ones_ref), custom_call_target="tpu_custom_call" | custom-call | tf_op jit(solution)/shard_map/height/pallas_call | solution.py:221
  55.4 0.0 copy-start.4
  55.4 24.3 %all_to_all.16 = bf16[32,32,512]{2,1,0:T(8,128)(2,1)S(1)} all-to-all(bf16[32,32,512]{2,1,0:T(8,128)(2,1)S(1)} %bitcast.7), channel_id=1, replica_groups=mesh['y'=4,'x'=4,'zh'=2,'zl'=4,'c'=2] {'y','x','c'}, dimensions={0} | all-to-all | bytes 2097152 | tf_op jit(solution)/shard_map/all_to_all | solution.py:232
  79.7 0.0 copy-done.5
  79.7 0.0 copy-done.4
  79.7 14.3 %depth.1 = bf16[1024,512]{1,0:T(8,128)(2,1)S(1)} custom-call(bf16[1024,512]{1,0:T(8,128)(2,1)S(1)} %bitcast.10, f32[4,512]{1,0:T(4,128)S(1)} %copy-done.8, bf16[3,512,1536]{2,1,0:T(8,128)(2,1)S(1)} %copy-done.1, bf16[3,512,512]{2,1,0:T(8,128)(2,1)S(1)} %copy-done.3, bf16[2,256,256]{2,1,0:T(8,128)(2,1)S(1)} %add_convert_fusion.ones_ref, ...), custom_call_target="tpu_custom_call" | custom-call | tf_op jit(solution)/shard_map/depth/pallas_call | solution.py:233
  94.0 37.4 %all_to_all.17 = bf16[128,8,512]{2,1,0:T(8,128)(2,1)S(1)} all-to-all(bf16[128,8,512]{2,1,0:T(8,128)(2,1)S(1)} %bitcast.11), channel_id=1, replica_groups=mesh['y'=4,'x'=4,'zh'=2,'zl'=4,'c'=2] {'y','x','zh','zl'}, dimensions={0} | all-to-all | bytes 2097152 | tf_op jit(solution)/shard_map/all_to_all | solution.py:244
  131.4 1.3 place.1
  (2 shorter events, 0.0 us)
Async XLA Ops:
  0.2 2.3 %copy-start = (bf16[3,512,1536]{2,1,0:T(8,128)(2,1)S(1)}, bf16[3,512,1536]{2,1,0:T(8,128)(2,1)}, u32[]{:S(2)}) copy-start(bf16[3,512,1536]{2,1,0:T(8,128)(2,1)} %qkv_ref.5) | copy-start | bytes 14155780
  2.5 1.4 %copy-start.2 = (bf16[3,512,512]{2,1,0:T(8,128)(2,1)S(1)}, bf16[3,512,512]{2,1,0:T(8,128)(2,1)}, u32[]{:S(2)}) copy-start(bf16[3,512,512]{2,1,0:T(8,128)(2,1)} %out_w_ref.5) | copy-start | bytes 4718596
  3.9 1.2 copy-start.6
  5.2 0.7 copy-start.7
  5.9 43.1 %copy-start.1 = (bf16[3,512,1536]{2,1,0:T(8,128)(2,1)S(1)}, bf16[3,512,1536]{2,1,0:T(8,128)(2,1)}, u32[]{:S(2)}) copy-start(bf16[3,512,1536]{2,1,0:T(8,128)(2,1)} %qkv_ref.5) | copy-start | bytes 14155780
  10.4 38.5 %copy-start.3 = (bf16[3,512,512]{2,1,0:T(8,128)(2,1)S(1)}, bf16[3,512,512]{2,1,0:T(8,128)(2,1)}, u32[]{:S(2)}) copy-start(bf16[3,512,512]{2,1,0:T(8,128)(2,1)} %out_w_ref.5) | copy-start | bytes 4718596
  10.5 38.5 %copy-start.8 = (f32[4,512]{1,0:T(4,128)S(1)}, f32[4,512]{1,0:T(4,128)}, u32[]{:S(2)}) copy-start(f32[4,512]{1,0:T(4,128)} %gain_ref.5) | copy-start | bytes 24580
  49.0 30.7 %copy-start.5 = (bf16[2048,512]{1,0:T(8,128)(2,1)S(1)}, bf16[2048,512]{1,0:T(8,128)(2,1)}, u32[]{:S(2)}) copy-start(bf16[2048,512]{1,0:T(8,128)(2,1)} %down_ref.1) | copy-start | bytes 6291460
  55.4 24.3 %copy-start.4 = (bf16[512,2048]{1,0:T(8,128)(2,1)S(1)}, bf16[512,2048]{1,0:T(8,128)(2,1)}, u32[]{:S(2)}) copy-start(bf16[512,2048]{1,0:T(8,128)(2,1)} %up_ref.1) | copy-start | bytes 6291460

commit v2 on v1

--- a/solution.py
+++ b/solution.py
@@ -1,5 +1,3 @@
-import functools
-
 import jax
 import jax.numpy as jnp
 from jax import lax
@@ -40,7 +38,15 @@
     return jnp.concatenate(parts, axis=1)
 
 
-def attend(x, gain, qkv_ref, out_ref, ones_ref):
+def ones_block(crossed):
+    row = lax.broadcasted_iota(jnp.int32, (256, 256), 0) // HEAD
+    column = lax.broadcasted_iota(jnp.int32, (256, 256), 1) // HEAD
+    if crossed:
+        column = column + 1 - 2 * (column % 2)
+    return jnp.where(row == column, 1.0, 0.0).astype(BF16)
+
+
+def attend(x, gain, qkv_ref, out_ref):
     n = x.shape[0] // LINE
     normed = layer_norm(x, gain)
     q = (dot(normed, qkv_ref[:, :D]) * (HEAD**-0.5)).astype(BF16)
@@ -91,7 +97,7 @@
                 e = softmax_top(scores, low)
                 exps[i].append(e)
                 mixed[i].append(dot(e, diagonal(first[2], second[2])))
-    sums = [dot(jnp.concatenate(exps[i], axis=0), ones_ref[i]) for i in range(2)]
+    sums = [dot(jnp.concatenate(exps[i], axis=0), ones_block(i)) for i in range(2)]
     rows = []
     for pair in range(n // 2):
         of_a, of_b = [], []
@@ -104,71 +110,79 @@
     return x + dot(jnp.concatenate(rows, axis=0), out_ref[...])
 
 
-def width_kernel(x_ref, gain_ref, qkv_ref, out_w_ref, ones_ref, y_ref):
+def width_kernel(x_hbm, gain_hbm, qkv_hbm, out_hbm, y_ref, x_ref, gain_ref, qkv_ref, out_ref, sems):
+    copies = [
+        pltpu.make_async_copy(source, target, sems.at[i])
+        for i, (source, target) in enumerate(
+            [(x_hbm, x_ref), (gain_hbm, gain_ref), (qkv_hbm.at[0], qkv_ref), (out_hbm.at[0], out_ref)]
+        )
+    ]
+    for copy in copies:
+        copy.start()
+    for copy in copies:
+        copy.wait()
     x = x_ref[...].reshape(TOKENS, D).astype(F32)
-    y = attend(x, gain_ref[0:1, :], qkv_ref, out_w_ref, ones_ref)
+    y = attend(x, gain_ref[0:1, :], qkv_ref, out_ref)
     for d in range(2):
         for z in range(8):
             pieces = [y[(d * 8 + h) * LINE + 8 * z :][:8] for h in range(8)]
             y_ref[z, d] = jnp.concatenate(pieces, axis=0).astype(BF16)
 
 
-def spread(x_ref, xs):
-    for c in range(4):
-        xs[c] = x_ref[:, c * 128 : (c + 1) * 128].astype(F32)
-
-
-def gather(ys, y_ref):
-    for c in range(4):
-        y_ref[:, c * 128 : (c + 1) * 128] = ys[c].astype(BF16)
-
-
-def take(xs, start, count, stride):
-    return jnp.concatenate([xs[c, pl.ds(start, count, stride=stride), :] for c in range(4)], axis=1)
-
-
-def put(ys, start, count, stride, value):
-    for c in range(4):
-        ys[c, pl.ds(start, count, stride=stride), :] = value[:, c * 128 : (c + 1) * 128]
-
-
-def height_kernel(x_ref, gain_ref, qkv_ref, out_w_ref, ones_ref, y_ref, xs, ys):
-    spread(x_ref, xs)
-    lines = [(zh, w) for zh in range(2) for w in range(8)]
-    x = jnp.concatenate([take(xs, zh * 512 + w, LINE, 8) for zh, w in lines], axis=0)
-    y = attend(x, gain_ref[1:2, :], qkv_ref, out_w_ref, ones_ref)
-    for n, (zh, w) in enumerate(lines):
-        for zl in range(4):
-            for c in range(2):
-                start = (w // 4) * 64 + c * 32 + zl * 8 + zh * 4 + w % 4
-                put(ys, start, 8, 128, y[n * LINE + (zl * 2 + c) * 8 :][:8])
-    gather(ys, y_ref)
-
-
-def depth_kernel(x_ref, gain_ref, qkv_ref, out_w_ref, ones_ref, up_ref, down_ref, y_ref, xs, ys):
-    spread(x_ref, xs)
-    lines = [(zl, w4) for zl in range(4) for w4 in range(4)]
-    quarters = [(zh, d0) for zh in range(2) for d0 in range(2)]
-    x = jnp.concatenate(
-        [
-            take(xs, d0 * 32 + zl * 8 + zh * 4 + w4, 16, 64)
-            for zl, w4 in lines
-            for zh, d0 in quarters
-        ],
-        axis=0,
-    )
-    x = attend(x, gain_ref[2:3, :], qkv_ref, out_w_ref, ones_ref)
+def turn(pieces):
+    turned = jnp.swapaxes(jnp.concatenate(pieces, axis=0).reshape(8, 8, D), 0, 1)
+    return [turned[i] for i in range(8)]
+
+
+def height_kernel(x_ref, gain_ref, qkv_ref, out_ref, y_ref):
+    x = x_ref[...].astype(F32).reshape(2, LINE, 8, D)
+    x = jnp.swapaxes(x, 1, 2).reshape(TOKENS, D)
+    y = attend(x, gain_ref[1:2, :], qkv_ref, out_ref)
+    for wsub in range(2):
+        for c in range(2):
+            tiles = [
+                turn(
+                    [
+                        y[((zh * 2 + wsub) * 4 + w4) * LINE + (zl * 2 + c) * 8 :][:8]
+                        for zh in range(2)
+                        for w4 in range(4)
+                    ]
+                )
+                for zl in range(4)
+            ]
+            for hs in range(8):
+                rows = jnp.concatenate([tiles[zl][hs] for zl in range(4)], axis=0)
+                y_ref[pl.ds(hs * 128 + wsub * 64 + c * 32, 32), :] = rows.astype(BF16)
+
+
+def depth_kernel(x_ref, gain_ref, qkv_ref, out_ref, up_ref, down_ref, y_ref):
+    x = x_ref[...].astype(F32)
+    pieces = {}
+    for yh in range(2):
+        for d0 in range(2):
+            for zl in range(4):
+                tile = [x[((yh * 8 + yl) * 2 + d0) * 32 + zl * 8 :][:8] for yl in range(8)]
+                for i, piece in enumerate(turn(tile)):
+                    pieces[zl, i % 4, i // 4, d0, yh] = piece
+    x = jnp.concatenate([pieces[key] for key in sorted(pieces)], axis=0)
+    x = attend(x, gain_ref[2:3, :], qkv_ref, out_ref)
     x = x.astype(BF16).astype(F32)
     normed = layer_norm(x, gain_ref[3:4, :])
     total = x
-    for part in range(4):
-        cols = slice(part * 512, (part + 1) * 512)
+    for part in range(2):
+        cols = slice(part * 1024, (part + 1) * 1024)
         hidden = jax.nn.gelu(dot(normed, up_ref[:, cols])).astype(BF16)
         total = total + dot(hidden, down_ref[cols, :])
-    for n, (zl, w4) in enumerate(lines):
-        for m, (zh, d0) in enumerate(quarters):
-            put(ys, zh * 32 + zl * 8 + d0 * 4 + w4, 16, 64, total[n * LINE + m * 16 :][:16])
-    gather(ys, y_ref)
+    pieces = {key: total[8 * i : 8 * i + 8] for i, key in enumerate(sorted(pieces))}
+    for zh in range(2):
+        for yh in range(2):
+            tiles = [
+                turn([pieces[zl, w4, zh, d0, yh] for d0 in range(2) for w4 in range(4)])
+                for zl in range(4)
+            ]
+            for yl in range(8):
+                rows = jnp.concatenate([tiles[zl][yl] for zl in range(4)], axis=0)
+                y_ref[pl.ds((yh * 8 + yl) * 64 + zh * 32, 32), :] = rows.astype(BF16)
 
 
 def place_kernel(x_ref, y_ref):
@@ -183,19 +197,11 @@
 PARAMS = pltpu.CompilerParams(vmem_limit_bytes=40 * 1024 * 1024)
 
 
-def ones_block():
-    head = jnp.arange(4 * HEAD) // HEAD
-    straight = head[:, None] == head[None, :]
-    crossed = head[:, None] == head[None, :] + 1 - 2 * (head[None, :] % 2)
-    return jnp.stack([straight, crossed]).astype(BF16)
-
-
 def weight_specs(layer):
     return [
         pl.BlockSpec((4, D), lambda *i: (0, 0)),
         pl.BlockSpec((None, D, 3 * D), lambda *i: (layer, 0, 0)),
         pl.BlockSpec((None, D, D), lambda *i: (layer, 0, 0)),
-        pl.BlockSpec((2, 4 * HEAD, 4 * HEAD), lambda *i: (0, 0, 0)),
     ]
 
 
@@ -204,27 +210,30 @@
 
 
 def body(volume, qkv_weight, out_weight, norm_gain, up_weight, down_weight):
-    ones = ones_block()
-    weights = (norm_gain, qkv_weight, out_weight, ones)
+    weights = (norm_gain, qkv_weight, out_weight)
     sent = pl.pallas_call(
         width_kernel,
-        grid=(1,),
-        in_specs=[whole(2, 8, LINE, D)] + weight_specs(0),
-        out_specs=whole(8, 2, 64, D),
+        in_specs=[pl.BlockSpec(memory_space=pltpu.HBM)] * 4,
+        out_specs=pl.BlockSpec(memory_space=pltpu.VMEM),
         out_shape=jax.ShapeDtypeStruct((8, 2, 64, D), BF16),
+        scratch_shapes=[
+            pltpu.VMEM((2, 8, LINE, D), BF16),
+            pltpu.VMEM((4, D), F32),
+            pltpu.VMEM((D, 3 * D), BF16),
+            pltpu.VMEM((D, D), BF16),
+            pltpu.SemaphoreType.DMA((4,)),
+        ],
         compiler_params=PARAMS,
         name="width",
-    )(volume, *weights)
+    )(*[pltpu.with_memory_space_constraint(a, pltpu.HBM) for a in (volume, *weights)])
     sent = sent.reshape(16, 64, D)
     held = lax.all_to_all(sent, ("zh", "zl", "c"), split_axis=0, concat_axis=0, tiled=True)
-    scratch = [pltpu.VMEM((4, TOKENS, 128), F32), pltpu.VMEM((4, TOKENS, 128), F32)]
     sent = pl.pallas_call(
         height_kernel,
         grid=(1,),
         in_specs=[whole(TOKENS, D)] + weight_specs(1),
         out_specs=whole(TOKENS, D),
         out_shape=jax.ShapeDtypeStruct((TOKENS, D), BF16),
-        scratch_shapes=scratch,
         compiler_params=PARAMS,
         name="height",
     )(held.reshape(TOKENS, D), *weights)
@@ -236,7 +245,6 @@
         in_specs=[whole(TOKENS, D)] + weight_specs(2) + [whole(D, FF), whole(FF, D)],
         out_specs=whole(TOKENS, D),
         out_shape=jax.ShapeDtypeStruct((TOKENS, D), BF16),
-        scratch_shapes=scratch,
         compiler_params=PARAMS,
         name="depth",
     )(held.reshape(TOKENS, D), *weights, up_weight, down_weight)

time: 133 us -> 124 us (0.932)
  local copies, waits for them, and re-layouts: 5.69 us -> 0.03 us
  Pallas kernels: 26.6 us -> 23.5 us
    unnamed x18 -> x10, local copies, waits for them, and re-layouts: 5.69 us -> 0.03 us
    pallas_call x1, Pallas kernels: 14.3 us -> 10.4 us  [body(): pl.pallas_call(depth_kernel, grid=(1,), in_specs=[whole(TOKENS, D)] + wei...]
    pallas_call x1, Pallas kernels: 4.57 us -> 6.65 us  [body(): pl.pallas_call(width_kernel, in_specs=[pl.BlockSpec(memory_space=pltpu.HB...]
where the time goes in v2:
time: 124 us
  blocking collectives  100 us (81%)
  Pallas kernels  23.5 us (19%)
    all_to_all x1, blocking collectives, body(): lax.all_to_all(sent, ('zh', 'zl', 'c'), split_axis=0, concat_axis=0, tile...  38.4 us
    all_to_all x1, blocking collectives, body(): lax.all_to_all(sent, ('y', 'x', 'zh', 'zl'), split_axis=0, concat_axis=0,...  37.4 us
    all_to_all x1, blocking collectives, body(): lax.all_to_all(sent, ('y', 'x', 'c'), split_axis=0, concat_axis=0, tiled=...  24.3 us
    pallas_call x1, Pallas kernels, body(): pl.pallas_call(depth_kernel, grid=(1,), in_specs=[whole(TOKENS, D)] + wei...  10.4 us
    pallas_call x1, Pallas kernels, body(): pl.pallas_call(width_kernel, in_specs=[pl.BlockSpec(memory_space=pltpu.HB...  6.65 us
    pallas_call x1, Pallas kernels, body(): pl.pallas_call(height_kernel, grid=(1,), in_specs=[whole(TOKENS, D)] + we...  5.16 us

profile of v2, /device:TPU:1, one launch (start us, length us, event | category | flops | bytes accessed | tf_op | source)
XLA Modules:
  0.0 123.7 jit_solution(5570211991000978784)
XLA Ops:
  0.0 0.0 copy-start
  0.0 6.6 %width.1 = bf16[8,2,64,512]{3,2,1,0:T(8,128)(2,1)S(1)} custom-call(bf16[2,8,64,512]{3,2,1,0:T(8,128)(2,1)} %x_hbm.1, f32[4,512]{1,0:T(4,128)} %gain_ref.3, bf16[3,512,1536]{2,1,0:T(8,128)(2,1)} %qkv_ref.3, bf16[3,512,512]{2,1,0:T(8,128)(2,1)} %out_ref.3), custom_call_target="tpu_custom_call" | custom-call | tf_op jit(solution)/shard_map/width/pallas_call | solution.py:214
  6.7 0.0 copy-start.1
  6.7 0.0 copy-start.4
  6.7 38.4 %all_to_all.15 = bf16[16,64,512]{2,1,0:T(8,128)(2,1)S(1)} all-to-all(bf16[16,64,512]{2,1,0:T(8,128)(2,1)S(1)} %bitcast.8), channel_id=1, replica_groups=mesh['y'=4,'x'=4,'zh'=2,'zl'=4,'c'=2] {'zh','zl','c'}, dimensions={0} | all-to-all | bytes 2097152 | tf_op jit(solution)/shard_map/all_to_all | solution.py:230
  45.1 0.0 copy-done
  45.1 0.0 copy-done.1
  45.1 0.0 copy-done.4
  45.1 0.0 copy-start.3
  45.2 5.2 %height.1 = bf16[1024,512]{1,0:T(8,128)(2,1)S(1)} custom-call(bf16[1024,512]{1,0:T(8,128)(2,1)S(1)} %bitcast.6, f32[4,512]{1,0:T(4,128)S(1)} %copy-done.4, bf16[3,512,1536]{2,1,0:T(8,128)(2,1)S(1)} %copy-done, bf16[3,512,512]{2,1,0:T(8,128)(2,1)S(1)} %copy-done.1), custom_call_target="tpu_custom_call" | custom-call | tf_op jit(solution)/shard_map/height/pallas_call | solution.py:231
  50.3 0.0 copy-start.2
  50.3 24.3 %all_to_all.16 = bf16[32,32,512]{2,1,0:T(8,128)(2,1)S(1)} all-to-all(bf16[32,32,512]{2,1,0:T(8,128)(2,1)S(1)} %bitcast.7), channel_id=1, replica_groups=mesh['y'=4,'x'=4,'zh'=2,'zl'=4,'c'=2] {'y','x','c'}, dimensions={0} | all-to-all | bytes 2097152 | tf_op jit(solution)/shard_map/all_to_all | solution.py:241
  74.6 0.0 copy-done.3
  74.6 0.0 copy-done.2
  74.6 10.4 %depth.1 = bf16[1024,512]{1,0:T(8,128)(2,1)S(1)} custom-call(bf16[1024,512]{1,0:T(8,128)(2,1)S(1)} %bitcast.10, f32[4,512]{1,0:T(4,128)S(1)} %copy-done.4, bf16[3,512,1536]{2,1,0:T(8,128)(2,1)S(1)} %copy-done, bf16[3,512,512]{2,1,0:T(8,128)(2,1)S(1)} %copy-done.1, bf16[512,2048]{1,0:T(8,128)(2,1)S(1)} %copy-done.2, bf16[2048,512]{1,0:T(8,128)(2,1)S(1)} %copy-done.3), custom_call_target="tpu_custom_call" | custom-call | tf_op jit(solution)/shard_map/depth/pallas_call | solution.py:242
  85.0 37.4 %all_to_all.17 = bf16[128,8,512]{2,1,0:T(8,128)(2,1)S(1)} all-to-all(bf16[128,8,512]{2,1,0:T(8,128)(2,1)S(1)} %bitcast.11), channel_id=1, replica_groups=mesh['y'=4,'x'=4,'zh'=2,'zl'=4,'c'=2] {'y','x','zh','zl'}, dimensions={0} | all-to-all | bytes 2097152 | tf_op jit(solution)/shard_map/all_to_all | solution.py:252
  122.4 1.3 %place.1 = bf16[2,8,64,512]{3,2,1,0:T(8,128)(2,1)} custom-call(bf16[8,2,64,512]{3,2,1,0:T(8,128)(2,1)S(1)} %bitcast.9), custom_call_target="tpu_custom_call" | custom-call | tf_op jit(solution)/shard_map/place/pallas_call | solution.py:253
Async XLA Ops:
  0.0 45.1 %copy-start = (bf16[3,512,1536]{2,1,0:T(8,128)(2,1)S(1)}, bf16[3,512,1536]{2,1,0:T(8,128)(2,1)}, u32[]{:S(2)}) copy-start(bf16[3,512,1536]{2,1,0:T(8,128)(2,1)} %qkv_ref.3) | copy-start | bytes 14155780
  6.7 38.5 %copy-start.1 = (bf16[3,512,512]{2,1,0:T(8,128)(2,1)S(1)}, bf16[3,512,512]{2,1,0:T(8,128)(2,1)}, u32[]{:S(2)}) copy-start(bf16[3,512,512]{2,1,0:T(8,128)(2,1)} %out_ref.3) | copy-start | bytes 4718596
  6.7 38.5 %copy-start.4 = (f32[4,512]{1,0:T(4,128)S(1)}, f32[4,512]{1,0:T(4,128)}, u32[]{:S(2)}) copy-start(f32[4,512]{1,0:T(4,128)} %gain_ref.3) | copy-start | bytes 24580
  45.1 29.5 %copy-start.3 = (bf16[2048,512]{1,0:T(8,128)(2,1)S(1)}, bf16[2048,512]{1,0:T(8,128)(2,1)}, u32[]{:S(2)}) copy-start(bf16[2048,512]{1,0:T(8,128)(2,1)} %down_ref.1) | copy-start | bytes 6291460
  50.3 24.3 %copy-start.2 = (bf16[512,2048]{1,0:T(8,128)(2,1)S(1)}, bf16[512,2048]{1,0:T(8,128)(2,1)}, u32[]{:S(2)}) copy-start(bf16[512,2048]{1,0:T(8,128)(2,1)} %up_ref.1) | copy-start | bytes 6291460

commit v3 on v2

--- a/solution.py
+++ b/solution.py
@@ -180,16 +180,18 @@
                 turn([pieces[zl, w4, zh, d0, yh] for d0 in range(2) for w4 in range(4)])
                 for zl in range(4)
             ]
-            for yl in range(8):
-                rows = jnp.concatenate([tiles[zl][yl] for zl in range(4)], axis=0)
-                y_ref[pl.ds((yh * 8 + yl) * 64 + zh * 32, 32), :] = rows.astype(BF16)
+            for y in range(2):
+                for zl in range(4):
+                    rows = jnp.concatenate(tiles[zl][4 * y : 4 * y + 4], axis=0)
+                    at = ((yh * 2 + y) * 8 + zh * 4 + zl) * 32
+                    y_ref[pl.ds(at, 32), :] = rows.astype(BF16)
 
 
 def place_kernel(x_ref, y_ref):
     low = lax.broadcasted_iota(jnp.int32, (LINE, D), 0) % 8 < 4
     for hs in range(8):
-        first = x_ref[hs, 0].astype(F32)
-        second = x_ref[hs, 1].astype(F32)
+        first = x_ref[hs // 2, :, hs % 2 * 2].reshape(LINE, D).astype(F32)
+        second = x_ref[hs // 2, :, hs % 2 * 2 + 1].reshape(LINE, D).astype(F32)
         y_ref[0, hs] = jnp.where(low, first, pltpu.roll(second, 4, 0)).astype(BF16)
         y_ref[1, hs] = jnp.where(low, pltpu.roll(first, LINE - 4, 0), second).astype(BF16)
 
@@ -249,16 +251,16 @@
         name="depth",
     )(held.reshape(TOKENS, D), *weights, up_weight, down_weight)
     sent = sent.reshape(128, 8, D)
-    held = lax.all_to_all(sent, ("y", "x", "zh", "zl"), split_axis=0, concat_axis=0, tiled=True)
+    held = lax.all_to_all(sent, ("y", "zh", "zl", "x"), split_axis=0, concat_axis=0, tiled=True)
     return pl.pallas_call(
         place_kernel,
         grid=(1,),
-        in_specs=[whole(8, 2, LINE, D)],
+        in_specs=[whole(4, 8, 4, 8, D)],
         out_specs=whole(2, 8, LINE, D),
         out_shape=jax.ShapeDtypeStruct((2, 8, LINE, D), BF16),
         compiler_params=PARAMS,
         name="place",
-    )(held.reshape(8, 2, LINE, D))
+    )(held.reshape(4, 8, 4, 8, D))
 
 
 def solution(mesh):

time: 124 us -> 121 us (0.976)
  blocking collectives: 100 us -> 97.7 us
    all_to_all x1, blocking collectives: 37.4 us -> 34.9 us  [body(): lax.all_to_all(sent, ('y', 'zh', 'zl', 'x'), split_axis=0, concat_axis=0,...]
where the time goes in v3:
time: 121 us
  blocking collectives  97.7 us (81%)
  Pallas kernels  23.5 us (19%)
    all_to_all x1, blocking collectives, body(): lax.all_to_all(sent, ('zh', 'zl', 'c'), split_axis=0, concat_axis=0, tile...  38.4 us
    all_to_all x1, blocking collectives, body(): lax.all_to_all(sent, ('y', 'zh', 'zl', 'x'), split_axis=0, concat_axis=0,...  34.9 us
    all_to_all x1, blocking collectives, body(): lax.all_to_all(sent, ('y', 'x', 'c'), split_axis=0, concat_axis=0, tiled=...  24.3 us
    pallas_call x1, Pallas kernels, body(): pl.pallas_call(depth_kernel, grid=(1,), in_specs=[whole(TOKENS, D)] + wei...  10.4 us
    pallas_call x1, Pallas kernels, body(): pl.pallas_call(width_kernel, in_specs=[pl.BlockSpec(memory_space=pltpu.HB...  6.65 us
    pallas_call x1, Pallas kernels, body(): pl.pallas_call(height_kernel, grid=(1,), in_specs=[whole(TOKENS, D)] + we...  5.16 us

profile of v3, /device:TPU:1, one launch (start us, length us, event | category | flops | bytes accessed | tf_op | source)
XLA Modules:
  0.0 121.2 jit_solution(7062276502932452268)
XLA Ops:
  0.0 0.0 copy-start
  0.0 6.6 %width.1 = bf16[8,2,64,512]{3,2,1,0:T(8,128)(2,1)S(1)} custom-call(bf16[2,8,64,512]{3,2,1,0:T(8,128)(2,1)} %x_hbm.1, f32[4,512]{1,0:T(4,128)} %gain_ref.3, bf16[3,512,1536]{2,1,0:T(8,128)(2,1)} %qkv_ref.3, bf16[3,512,512]{2,1,0:T(8,128)(2,1)} %out_ref.3), custom_call_target="tpu_custom_call" | custom-call | tf_op jit(solution)/shard_map/width/pallas_call | solution.py:216
  6.7 0.0 copy-start.1
  6.7 0.0 copy-start.4
  6.7 38.4 %all_to_all.15 = bf16[16,64,512]{2,1,0:T(8,128)(2,1)S(1)} all-to-all(bf16[16,64,512]{2,1,0:T(8,128)(2,1)S(1)} %bitcast.8), channel_id=1, replica_groups=mesh['y'=4,'x'=4,'zh'=2,'zl'=4,'c'=2] {'zh','zl','c'}, dimensions={0} | all-to-all | bytes 2097152 | tf_op jit(solution)/shard_map/all_to_all | solution.py:232
  45.1 0.0 copy-done
  45.1 0.0 copy-done.1
  45.1 0.0 copy-done.4
  45.1 0.0 copy-start.3
  45.2 5.2 %height.1 = bf16[1024,512]{1,0:T(8,128)(2,1)S(1)} custom-call(bf16[1024,512]{1,0:T(8,128)(2,1)S(1)} %bitcast.6, f32[4,512]{1,0:T(4,128)S(1)} %copy-done.4, bf16[3,512,1536]{2,1,0:T(8,128)(2,1)S(1)} %copy-done, bf16[3,512,512]{2,1,0:T(8,128)(2,1)S(1)} %copy-done.1), custom_call_target="tpu_custom_call" | custom-call | tf_op jit(solution)/shard_map/height/pallas_call | solution.py:233
  50.3 0.0 copy-start.2
  50.3 24.3 %all_to_all.16 = bf16[32,32,512]{2,1,0:T(8,128)(2,1)S(1)} all-to-all(bf16[32,32,512]{2,1,0:T(8,128)(2,1)S(1)} %bitcast.7), channel_id=1, replica_groups=mesh['y'=4,'x'=4,'zh'=2,'zl'=4,'c'=2] {'y','x','c'}, dimensions={0} | all-to-all | bytes 2097152 | tf_op jit(solution)/shard_map/all_to_all | solution.py:243
  74.6 0.0 copy-done.3
  74.6 0.0 copy-done.2
  74.6 10.4 %depth.1 = bf16[1024,512]{1,0:T(8,128)(2,1)S(1)} custom-call(bf16[1024,512]{1,0:T(8,128)(2,1)S(1)} %bitcast.10, f32[4,512]{1,0:T(4,128)S(1)} %copy-done.4, bf16[3,512,1536]{2,1,0:T(8,128)(2,1)S(1)} %copy-done, bf16[3,512,512]{2,1,0:T(8,128)(2,1)S(1)} %copy-done.1, bf16[512,2048]{1,0:T(8,128)(2,1)S(1)} %copy-done.2, bf16[2048,512]{1,0:T(8,128)(2,1)S(1)} %copy-done.3), custom_call_target="tpu_custom_call" | custom-call | tf_op jit(solution)/shard_map/depth/pallas_call | solution.py:244
  85.0 34.9 %all_to_all.17 = bf16[128,8,512]{2,1,0:T(8,128)(2,1)S(1)} all-to-all(bf16[128,8,512]{2,1,0:T(8,128)(2,1)S(1)} %bitcast.11), channel_id=1, replica_groups=mesh['y'=4,'x'=4,'zh'=2,'zl'=4,'c'=2] {'y','zh','zl','x'}, dimensions={0} | all-to-all | bytes 2097152 | tf_op jit(solution)/shard_map/all_to_all | solution.py:254
  119.9 1.3 %place.1 = bf16[2,8,64,512]{3,2,1,0:T(8,128)(2,1)} custom-call(bf16[4,8,4,8,512]{4,3,2,1,0:T(8,128)(2,1)S(1)} %bitcast.9), custom_call_target="tpu_custom_call" | custom-call | tf_op jit(solution)/shard_map/place/pallas_call | solution.py:255
Async XLA Ops:
  0.0 45.1 %copy-start = (bf16[3,512,1536]{2,1,0:T(8,128)(2,1)S(1)}, bf16[3,512,1536]{2,1,0:T(8,128)(2,1)}, u32[]{:S(2)}) copy-start(bf16[3,512,1536]{2,1,0:T(8,128)(2,1)} %qkv_ref.3) | copy-start | bytes 14155780
  6.7 38.5 %copy-start.1 = (bf16[3,512,512]{2,1,0:T(8,128)(2,1)S(1)}, bf16[3,512,512]{2,1,0:T(8,128)(2,1)}, u32[]{:S(2)}) copy-start(bf16[3,512,512]{2,1,0:T(8,128)(2,1)} %out_ref.3) | copy-start | bytes 4718596
  6.7 38.5 %copy-start.4 = (f32[4,512]{1,0:T(4,128)S(1)}, f32[4,512]{1,0:T(4,128)}, u32[]{:S(2)}) copy-start(f32[4,512]{1,0:T(4,128)} %gain_ref.3) | copy-start | bytes 24580
  45.1 29.5 %copy-start.3 = (bf16[2048,512]{1,0:T(8,128)(2,1)S(1)}, bf16[2048,512]{1,0:T(8,128)(2,1)}, u32[]{:S(2)}) copy-start(bf16[2048,512]{1,0:T(8,128)(2,1)} %down_ref.1) | copy-start | bytes 6291460
  50.3 24.3 %copy-start.2 = (bf16[512,2048]{1,0:T(8,128)(2,1)S(1)}, bf16[512,2048]{1,0:T(8,128)(2,1)}, u32[]{:S(2)}) copy-start(bf16[512,2048]{1,0:T(8,128)(2,1)} %up_ref.1) | copy-start | bytes 6291460

commit v4 on v3

--- a/solution.py
+++ b/solution.py
@@ -110,23 +110,45 @@
     return x + dot(jnp.concatenate(rows, axis=0), out_ref[...])
 
 
-def width_kernel(x_hbm, gain_hbm, qkv_hbm, out_hbm, y_ref, x_ref, gain_ref, qkv_ref, out_ref, sems):
+def own_z():
+    return lax.axis_index("zh") * 4 + lax.axis_index("zl")
+
+
+def by_distance(y, y_ref):
+    here = own_z()
+    for z in range(8):
+        pieces = [y[h * LINE + 8 * z :][:8] for h in range(8)]
+        y_ref[lax.rem(z + 8 - here, 8)] = jnp.concatenate(pieces, axis=0).astype(BF16)
+
+
+def width_away_kernel(
+    x_hbm, gain_hbm, qkv_hbm, out_hbm, y_ref, home_ref, gain_ref, qkv_ref, out_ref, x_ref, sems
+):
+    core = lax.axis_index("c")
     copies = [
         pltpu.make_async_copy(source, target, sems.at[i])
         for i, (source, target) in enumerate(
-            [(x_hbm, x_ref), (gain_hbm, gain_ref), (qkv_hbm.at[0], qkv_ref), (out_hbm.at[0], out_ref)]
+            [
+                (x_hbm.at[1 - core], x_ref),
+                (gain_hbm, gain_ref),
+                (qkv_hbm.at[0], qkv_ref),
+                (out_hbm.at[0], out_ref),
+                (x_hbm.at[core], home_ref),
+            ]
         )
     ]
     for copy in copies:
         copy.start()
-    for copy in copies:
+    for copy in copies[:4]:
         copy.wait()
-    x = x_ref[...].reshape(TOKENS, D).astype(F32)
-    y = attend(x, gain_ref[0:1, :], qkv_ref, out_ref)
-    for d in range(2):
-        for z in range(8):
-            pieces = [y[(d * 8 + h) * LINE + 8 * z :][:8] for h in range(8)]
-            y_ref[z, d] = jnp.concatenate(pieces, axis=0).astype(BF16)
+    x = x_ref[...].reshape(8 * LINE, D).astype(F32)
+    by_distance(attend(x, gain_ref[0:1, :], qkv_ref, out_ref), y_ref)
+    copies[4].wait()
+
+
+def width_home_kernel(x_ref, gain_ref, qkv_ref, out_ref, y_ref):
+    x = x_ref[...].reshape(8 * LINE, D).astype(F32)
+    by_distance(attend(x, gain_ref[0:1, :], qkv_ref, out_ref), y_ref)
 
 
 def turn(pieces):
@@ -134,7 +156,12 @@
     return [turned[i] for i in range(8)]
 
 
-def height_kernel(x_ref, gain_ref, qkv_ref, out_ref, y_ref):
+def height_kernel(*refs):
+    *blocks, gain_ref, qkv_ref, out_ref, y_ref, x_ref = refs
+    here, own_core = own_z(), lax.axis_index("c")
+    for distance, block in zip(DISTANCES, blocks):
+        for core in range(2):
+            x_ref[lax.rem(here + 8 - distance, 8), lax.bitwise_xor(own_core, core)] = block[core]
     x = x_ref[...].astype(F32).reshape(2, LINE, 8, D)
     x = jnp.swapaxes(x, 1, 2).reshape(TOKENS, D)
     y = attend(x, gain_ref[1:2, :], qkv_ref, out_ref)
@@ -197,6 +224,9 @@
 
 
 PARAMS = pltpu.CompilerParams(vmem_limit_bytes=40 * 1024 * 1024)
+DISTANCES = (0, 1, 7, 3, 5, 4, 2, 6)
+IN_HBM = pl.BlockSpec(memory_space=pltpu.HBM)
+IN_VMEM = pl.BlockSpec(memory_space=pltpu.VMEM)
 
 
 def weight_specs(layer):
@@ -211,34 +241,55 @@
     return pl.BlockSpec(shape, lambda *i: (0,) * len(shape))
 
 
+def cost(nanoseconds):
+    return pl.CostEstimate(flops=700_000 * nanoseconds, bytes_accessed=1 << 20, transcendentals=0)
+
+
+def phase(kernel, shape, *operands, **options):
+    return pl.pallas_call(
+        kernel,
+        in_specs=[IN_VMEM] * len(operands),
+        out_specs=IN_VMEM,
+        out_shape=jax.ShapeDtypeStruct(shape, BF16),
+        compiler_params=PARAMS,
+        **options,
+    )(*operands)
+
+
 def body(volume, qkv_weight, out_weight, norm_gain, up_weight, down_weight):
     weights = (norm_gain, qkv_weight, out_weight)
-    sent = pl.pallas_call(
-        width_kernel,
-        in_specs=[pl.BlockSpec(memory_space=pltpu.HBM)] * 4,
-        out_specs=pl.BlockSpec(memory_space=pltpu.VMEM),
-        out_shape=jax.ShapeDtypeStruct((8, 2, 64, D), BF16),
-        scratch_shapes=[
-            pltpu.VMEM((2, 8, LINE, D), BF16),
-            pltpu.VMEM((4, D), F32),
-            pltpu.VMEM((D, 3 * D), BF16),
-            pltpu.VMEM((D, D), BF16),
-            pltpu.SemaphoreType.DMA((4,)),
+    half = (8, LINE, D)
+    away, home, *first_weights = pl.pallas_call(
+        width_away_kernel,
+        in_specs=[IN_HBM] * 4,
+        out_specs=[IN_VMEM] * 5,
+        out_shape=[
+            jax.ShapeDtypeStruct(half, BF16),
+            jax.ShapeDtypeStruct(half, BF16),
+            jax.ShapeDtypeStruct((4, D), F32),
+            jax.ShapeDtypeStruct((D, 3 * D), BF16),
+            jax.ShapeDtypeStruct((D, D), BF16),
         ],
-        compiler_params=PARAMS,
-        name="width",
+        scratch_shapes=[pltpu.VMEM(half, BF16), pltpu.SemaphoreType.DMA((5,))],
+        compiler_params=PARAMS,
+        name="width_away",
     )(*[pltpu.with_memory_space_constraint(a, pltpu.HBM) for a in (volume, *weights)])
-    sent = sent.reshape(16, 64, D)
-    held = lax.all_to_all(sent, ("zh", "zl", "c"), split_axis=0, concat_axis=0, tiled=True)
+    away = lax.ppermute(away, "c", [(0, 1), (1, 0)])
+    home = phase(width_home_kernel, half, home, *first_weights, name="width_home", cost_estimate=cost(3000))
+    blocks = [jnp.stack([home[i], away[i]]) for i in range(8)]
+    held = blocks[:1] + [
+        lax.ppermute(blocks[i], ("zh", "zl"), [(z, (z + i) % 8) for z in range(8)]) for i in DISTANCES[1:]
+    ]
     sent = pl.pallas_call(
         height_kernel,
         grid=(1,),
-        in_specs=[whole(TOKENS, D)] + weight_specs(1),
+        in_specs=[whole(2, LINE, D)] * 8 + weight_specs(1),
         out_specs=whole(TOKENS, D),
         out_shape=jax.ShapeDtypeStruct((TOKENS, D), BF16),
+        scratch_shapes=[pltpu.VMEM((8, 2, LINE, D), BF16)],
         compiler_params=PARAMS,
         name="height",
-    )(held.reshape(TOKENS, D), *weights)
+    )(*held, *weights)
     sent = sent.reshape(32, 32, D)
     held = lax.all_to_all(sent, ("y", "x", "c"), split_axis=0, concat_axis=0, tiled=True)
     sent = pl.pallas_call(

time: 121 us -> 120 us (level)
  blocking collectives: 97.7 us -> 63.9 us
  starting transfers between devices: 0 us -> 19.7 us
  waiting for transfers between devices: 0 us -> 11.6 us
    all_to_all x1 -> x0, blocking collectives: 38.4 us -> none  [body(): lax.all_to_all(sent, ('zh', 'zl', 'c'), split_axis=0, concat_axis=0, tile...]
    ppermute x0 -> x8, starting transfers between devices: none -> 19.7 us  [the longest x7 16.3 us: body(): lax.ppermute(blocks[i], ('zh', 'zl'), [(z, (z + i) % 8) for z in range(8)])]
    ppermute x0 -> x8, waiting for transfers between devices: none -> 11.6 us  [the longest x7 11.6 us: body(): lax.ppermute(blocks[i], ('zh', 'zl'), [(z, (z + i) % 8) for z in range(8)])]
    all_to_all x1, blocking collectives: 34.9 us -> 38.7 us  [body(): lax.all_to_all(sent, ('y', 'zh', 'zl', 'x'), split_axis=0, concat_axis=0,...]
    pallas_call x2 -> x3, Pallas kernels: 11.8 us -> 12.1 us  [the longest x1 5.23 us: body(): pl.pallas_call(height_kernel, grid=(1,), in_specs=[whole(2, LINE, D)] * 8...]
  transfers between devices with their start and end apart: 0 -> 8, of which waited for: 0 -> 3; matrix products, arithmetic and copies ran while one was open for 0% -> 0% of each run, Pallas kernels for 0% -> 2%
where the time goes in v4:
time: 120 us; the launch traced here: 119 us
  blocking collectives  63.9 us (53%)
  Pallas kernels  23.8 us (20%)
  starting transfers between devices  19.7 us (16%)
  waiting for transfers between devices  11.6 us (10%)
    all_to_all x1, blocking collectives, body(): lax.all_to_all(sent, ('y', 'zh', 'zl', 'x'), split_axis=0, concat_axis=0,...  38.7 us
    all_to_all x1, blocking collectives, body(): lax.all_to_all(sent, ('y', 'x', 'c'), split_axis=0, concat_axis=0, tiled=...  25.2 us
    ppermute x7, starting transfers between devices, body(): lax.ppermute(blocks[i], ('zh', 'zl'), [(z, (z + i) % 8) for z in range(8)])  16.3 us
    ppermute x7, waiting for transfers between devices, body(): lax.ppermute(blocks[i], ('zh', 'zl'), [(z, (z + i) % 8) for z in range(8)])  11.6 us
    pallas_call x1, Pallas kernels, body(): pl.pallas_call(depth_kernel, grid=(1,), in_specs=[whole(TOKENS, D)] + wei...  10.4 us
    pallas_call x1, Pallas kernels, body(): pl.pallas_call(height_kernel, grid=(1,), in_specs=[whole(2, LINE, D)] * 8...  5.23 us
    pallas_call x1, Pallas kernels, body(): pl.pallas_call(width_away_kernel, in_specs=[IN_HBM] * 4, out_specs=[IN_VM...  4.32 us
    ppermute x1, starting transfers between devices, body(): away = lax.ppermute(away, 'c', [(0, 1), (1, 0)])  3.33 us
  transfers between devices with their start and end apart: 8, of which 3 were waited for; matrix products, arithmetic and copies ran while one was open for 0% of the time, Pallas kernels for 2%

profile of v4, /device:TPU:1, one launch (start us, length us, event | category | flops | bytes accessed | tf_op | source)
XLA Modules:
  0.0 119.4 jit_solution(2218384092188202395)
XLA Ops:
  0.0 4.3 %width_away.1 = (bf16[8,64,512]{2,1,0:T(8,128)(2,1)S(1)}, bf16[8,64,512]{2,1,0:T(8,128)(2,1)S(1)}, f32[4,512]{1,0:T(4,128)S(1)}, bf16[512,1536]{1,0:T(8,128)(2,1)S(1)}, bf16[512,512]{1,0:T(8,128)(2,1)S(1)}) custom-call(bf16[2,8,64,512]{3,2,1,0:T(8,128)(2,1)} %x_hbm.1, f32[4,512]{1,0:T(4,128)} %gain_ref.1, bf16[3,512,1536]{2,1,0:T(8,128)(2,1)} %qkv_ref.1, ...), custom_call_target="tpu_custom_call" | custom-call | tf_op jit(solution)/shard_map/width_away/pallas_call | solution.py:262
  4.3 3.3 %collective-permute-start = (bf16[8,64,512]{2,1,0:T(8,128)(2,1)S(1)}, bf16[8,64,512]{2,1,0:T(8,128)(2,1)S(1)}, u32[]{:S(2)}, u32[]{:S(2)}) collective-permute-start(bf16[8,64,512]{2,1,0:T(8,128)(2,1)S(1)} %get-tuple-element.14), channel_id=1, source_target_pairs={{0,1},{1,0},{2,3},{3,2},{4,5},{5,4},{6,7},{7,6},{8,9},{9,8},{10,11... | collective-permute-start | bytes 1572872 | tf_op jit(solution)/shard_map/ppermute | solution.py:277
  7.7 0.0 slice-start
  7.7 0.0 slice-start.1
  7.7 2.6 %width_home.1 = bf16[8,64,512]{2,1,0:T(8,128)(2,1)S(1)} custom-call(bf16[8,64,512]{2,1,0:T(8,128)(2,1)S(1)} %get-tuple-element.10.x_ref, f32[4,512]{1,0:T(4,128)S(1)} %get-tuple-element.11.gain_ref, bf16[512,1536]{1,0:T(8,128)(2,1)S(1)} %get-tuple-element.12.qkv_ref, bf16[512,512]{1,0:T(8,128)(2,1)S(1)} %get-tuple-element.13.out_ref), custom_call_target="tpu_custom_call" | custom-call | flops 2100000000 | bytes 1048576 | tf_op jit(solution)/shard_map/width_home/pallas_call | solution.py:249
  10.3 0.0 copy-start
  10.3 0.0 copy-start.3
  10.3 0.0 collective-permute-done
  10.4 0.1 collective-permute-start.1
  10.5 3.9 %collective-permute-start.2 = (bf16[2,64,512]{2,1,0:T(8,128)(2,1)S(1)}, bf16[2,64,512]{2,1,0:T(8,128)(2,1)S(1)}, u32[]{:S(2)}, u32[]{:S(2)}) collective-permute-start(bf16[2,64,512]{2,1,0:T(8,128)(2,1)S(1)} %pad_maximum_fusion.2), channel_id=1, source_target_pairs={{0,14},{2,0},{4,2},{6,4},{8,6},{10,8},{12,10},{14,12},{1,15},{3,1}... | collective-permute-start | bytes 393224 | tf_op jit(solution)/shard_map/ppermute | solution.py:281
  14.5 1.7 %collective-permute-start.3 = (bf16[2,64,512]{2,1,0:T(8,128)(2,1)S(1)}, bf16[2,64,512]{2,1,0:T(8,128)(2,1)S(1)}, u32[]{:S(2)}, u32[]{:S(2)}) collective-permute-start(bf16[2,64,512]{2,1,0:T(8,128)(2,1)S(1)} %pad_maximum_fusion.3), channel_id=1, source_target_pairs={{0,6},{2,8},{4,10},{6,12},{8,14},{10,0},{12,2},{14,4},{1,7},{3,9},... | collective-permute-start | bytes 393224 | tf_op jit(solution)/shard_map/ppermute | solution.py:281
  16.2 2.9 %collective-permute-start.4 = (bf16[2,64,512]{2,1,0:T(8,128)(2,1)S(1)}, bf16[2,64,512]{2,1,0:T(8,128)(2,1)S(1)}, u32[]{:S(2)}, u32[]{:S(2)}) collective-permute-start(bf16[2,64,512]{2,1,0:T(8,128)(2,1)S(1)} %pad_maximum_fusion.4), channel_id=1, source_target_pairs={{0,10},{2,12},{4,14},{6,0},{8,2},{10,4},{12,6},{14,8},{1,11},{3,13... | collective-permute-start | bytes 393224 | tf_op jit(solution)/shard_map/ppermute | solution.py:281
  19.1 4.1 %collective-permute-start.5 = (bf16[2,64,512]{2,1,0:T(8,128)(2,1)S(1)}, bf16[2,64,512]{2,1,0:T(8,128)(2,1)S(1)}, u32[]{:S(2)}, u32[]{:S(2)}) collective-permute-start(bf16[2,64,512]{2,1,0:T(8,128)(2,1)S(1)} %pad_maximum_fusion.5), channel_id=1, source_target_pairs={{0,8},{2,10},{4,12},{6,14},{8,0},{10,2},{12,4},{14,6},{1,9},{3,11}... | collective-permute-start | bytes 393224 | tf_op jit(solution)/shard_map/ppermute | solution.py:281
  23.2 0.0 collective-permute-done.1.refs_1_
  23.3 0.1 collective-permute-start.6
  23.3 0.0 collective-permute-done.2.refs_2_
  23.4 3.6 %collective-permute-start.7 = (bf16[2,64,512]{2,1,0:T(8,128)(2,1)S(1)}, bf16[2,64,512]{2,1,0:T(8,128)(2,1)S(1)}, u32[]{:S(2)}, u32[]{:S(2)}) collective-permute-start(bf16[2,64,512]{2,1,0:T(8,128)(2,1)S(1)} %pad_maximum_fusion.7), channel_id=1, source_target_pairs={{0,12},{2,14},{4,0},{6,2},{8,4},{10,6},{12,8},{14,10},{1,13},{3,15... | collective-permute-start | bytes 393224 | tf_op jit(solution)/shard_map/ppermute | solution.py:281
  26.9 0.0 collective-permute-done.3.refs_3_
  26.9 0.0 collective-permute-done.4.refs_4_
  26.9 5.0 %collective-permute-done.5.refs_5_ = bf16[2,64,512]{2,1,0:T(8,128)(2,1)S(1)} collective-permute-done((bf16[2,64,512]{2,1,0:T(8,128)(2,1)S(1)}, bf16[2,64,512]{2,1,0:T(8,128)(2,1)S(1)}, u32[]{:S(2)}, u32[]{:S(2)}) %collective-permute-start.5) | collective-permute-done | bytes 131104 | tf_op jit(solution)/shard_map/ppermute | solution.py:281
  32.0 5.8 %collective-permute-done.6.refs_6_ = bf16[2,64,512]{2,1,0:T(8,128)(2,1)S(1)} collective-permute-done((bf16[2,64,512]{2,1,0:T(8,128)(2,1)S(1)}, bf16[2,64,512]{2,1,0:T(8,128)(2,1)S(1)}, u32[]{:S(2)}, u32[]{:S(2)}) %collective-permute-start.6) | collective-permute-done | bytes 131104 | tf_op jit(solution)/shard_map/ppermute | solution.py:281
  37.8 0.7 collective-permute-done.7.refs_7_
  38.5 0.0 slice-done
  38.5 0.0 slice-done.1
  38.5 0.0 copy-done
  38.5 0.0 copy-done.3
  38.6 0.0 copy-start.2
  38.6 5.2 %height.1 = bf16[1024,512]{1,0:T(8,128)(2,1)S(1)} custom-call(bf16[2,64,512]{2,1,0:T(8,128)(2,1)S(1)} %pad_maximum_fusion.refs_0_, bf16[2,64,512]{2,1,0:T(8,128)(2,1)S(1)} %collective-permute-done.1.refs_1_, bf16[2,64,512]{2,1,0:T(8,128)(2,1)S(1)} %collective-permute-done.2.refs_2_, bf16[2,64,512]{2,1,0:T(8,128)(2,1)S(1)} %collective-permute-done.3.refs_3_, ...), custom_call_target="tpu_custom_call" | custom-call | tf_op jit(solution)/shard_map/height/pallas_call | solution.py:283
  43.8 0.0 copy-start.1
  43.8 25.2 %all_to_all.10 = bf16[32,32,512]{2,1,0:T(8,128)(2,1)S(1)} all-to-all(bf16[32,32,512]{2,1,0:T(8,128)(2,1)S(1)} %bitcast.6), channel_id=1, replica_groups=mesh['y'=4,'x'=4,'zh'=2,'zl'=4,'c'=2] {'y','x','c'}, dimensions={0} | all-to-all | bytes 2097152 | tf_op jit(solution)/shard_map/all_to_all | solution.py:294
  69.0 0.0 copy-done.2
  69.0 0.0 copy-done.1
  69.0 10.4 %depth.1 = bf16[1024,512]{1,0:T(8,128)(2,1)S(1)} custom-call(bf16[1024,512]{1,0:T(8,128)(2,1)S(1)} %bitcast.8, f32[4,512]{1,0:T(4,128)S(1)} %copy-done.3, bf16[3,512,1536]{2,1,0:T(8,128)(2,1)S(1)} %bitcast.5, bf16[3,512,512]{2,1,0:T(8,128)(2,1)S(1)} %copy-done, bf16[512,2048]{1,0:T(8,128)(2,1)S(1)} %copy-done.1, bf16[2048,512]{1,0:T(8,128)(2,1)S(1)} %copy-done.2), custom_call_target="tpu_custom_call" | custom-call | tf_op jit(solution)/shard_map/depth/pallas_call | solution.py:295
  79.4 38.7 %all_to_all.11 = bf16[128,8,512]{2,1,0:T(8,128)(2,1)S(1)} all-to-all(bf16[128,8,512]{2,1,0:T(8,128)(2,1)S(1)} %bitcast.9), channel_id=1, replica_groups=mesh['y'=4,'x'=4,'zh'=2,'zl'=4,'c'=2] {'y','zh','zl','x'}, dimensions={0} | all-to-all | bytes 2097152 | tf_op jit(solution)/shard_map/all_to_all | solution.py:305
  118.1 1.3 %place.1 = bf16[2,8,64,512]{3,2,1,0:T(8,128)(2,1)} custom-call(bf16[4,8,4,8,512]{4,3,2,1,0:T(8,128)(2,1)S(1)} %bitcast.7), custom_call_target="tpu_custom_call" | custom-call | tf_op jit(solution)/shard_map/place/pallas_call | solution.py:306
  (11 shorter events, 0.2 us)
Async XLA Ops:
  4.3 6.0 %collective-permute-start = (bf16[8,64,512]{2,1,0:T(8,128)(2,1)S(1)}, bf16[8,64,512]{2,1,0:T(8,128)(2,1)S(1)}, u32[]{:S(2)}, u32[]{:S(2)}) collective-permute-start(bf16[8,64,512]{2,1,0:T(8,128)(2,1)S(1)} %get-tuple-element.14), channel_id=1, source_target_pairs={{0,1},{1,0},{2,3},{3,2},{4,5},{5,4},{6,7},{7,6},{8,9},{9,8},{10,11... | collective-permute-start | bytes 1572872 | tf_op jit(solution)/shard_map/ppermute | solution.py:277
  7.7 30.9 %slice-start = ((s8[4718592]{0:T(1024)(128)(4,1)}), s8[4194304]{0:T(1024)(128)(4,1)S(1)}, s32[]{:S(2)}) async-start(s8[4718592]{0:T(1024)(128)(4,1)} %bitcast.4), calls=%async_computation.2 | async-start | bytes 8388608
  7.7 30.9 %slice-start.1 = ((s8[4718592]{0:T(1024)(128)(4,1)}), s8[524288]{0:T(1024)(128)(4,1)S(1)}, s32[]{:S(2)}) async-start(s8[4718592]{0:T(1024)(128)(4,1)} %bitcast.4), calls=%async_computation.3 | async-start | bytes 1048576
  10.3 28.3 %copy-start = (bf16[3,512,512]{2,1,0:T(8,128)(2,1)S(1)}, bf16[3,512,512]{2,1,0:T(8,128)(2,1)}, u32[]{:S(2)}) copy-start(bf16[3,512,512]{2,1,0:T(8,128)(2,1)} %out_ref.1) | copy-start | bytes 4718596
  10.3 28.3 %copy-start.3 = (f32[4,512]{1,0:T(4,128)S(1)}, f32[4,512]{1,0:T(4,128)}, u32[]{:S(2)}) copy-start(f32[4,512]{1,0:T(4,128)} %gain_ref.1) | copy-start | bytes 24580
  10.4 12.8 %collective-permute-start.1 = (bf16[2,64,512]{2,1,0:T(8,128)(2,1)S(1)}, bf16[2,64,512]{2,1,0:T(8,128)(2,1)S(1)}, u32[]{:S(2)}, u32[]{:S(2)}) collective-permute-start(bf16[2,64,512]{2,1,0:T(8,128)(2,1)S(1)} %pad_maximum_fusion.1), channel_id=1, source_target_pairs={{0,2},{2,4},{4,6},{6,8},{8,10},{10,12},{12,14},{14,0},{1,3},{3,5},... | collective-permute-start | bytes 393224 | tf_op jit(solution)/shard_map/ppermute | solution.py:281
  10.5 12.8 %collective-permute-start.2 = (bf16[2,64,512]{2,1,0:T(8,128)(2,1)S(1)}, bf16[2,64,512]{2,1,0:T(8,128)(2,1)S(1)}, u32[]{:S(2)}, u32[]{:S(2)}) collective-permute-start(bf16[2,64,512]{2,1,0:T(8,128)(2,1)S(1)} %pad_maximum_fusion.2), channel_id=1, source_target_pairs={{0,14},{2,0},{4,2},{6,4},{8,6},{10,8},{12,10},{14,12},{1,15},{3,1}... | collective-permute-start | bytes 393224 | tf_op jit(solution)/shard_map/ppermute | solution.py:281
  14.5 12.5 %collective-permute-start.3 = (bf16[2,64,512]{2,1,0:T(8,128)(2,1)S(1)}, bf16[2,64,512]{2,1,0:T(8,128)(2,1)S(1)}, u32[]{:S(2)}, u32[]{:S(2)}) collective-permute-start(bf16[2,64,512]{2,1,0:T(8,128)(2,1)S(1)} %pad_maximum_fusion.3), channel_id=1, source_target_pairs={{0,6},{2,8},{4,10},{6,12},{8,14},{10,0},{12,2},{14,4},{1,7},{3,9},... | collective-permute-start | bytes 393224 | tf_op jit(solution)/shard_map/ppermute | solution.py:281
  16.2 10.8 %collective-permute-start.4 = (bf16[2,64,512]{2,1,0:T(8,128)(2,1)S(1)}, bf16[2,64,512]{2,1,0:T(8,128)(2,1)S(1)}, u32[]{:S(2)}, u32[]{:S(2)}) collective-permute-start(bf16[2,64,512]{2,1,0:T(8,128)(2,1)S(1)} %pad_maximum_fusion.4), channel_id=1, source_target_pairs={{0,10},{2,12},{4,14},{6,0},{8,2},{10,4},{12,6},{14,8},{1,11},{3,13... | collective-permute-start | bytes 393224 | tf_op jit(solution)/shard_map/ppermute | solution.py:281
  19.1 12.8 %collective-permute-start.5 = (bf16[2,64,512]{2,1,0:T(8,128)(2,1)S(1)}, bf16[2,64,512]{2,1,0:T(8,128)(2,1)S(1)}, u32[]{:S(2)}, u32[]{:S(2)}) collective-permute-start(bf16[2,64,512]{2,1,0:T(8,128)(2,1)S(1)} %pad_maximum_fusion.5), channel_id=1, source_target_pairs={{0,8},{2,10},{4,12},{6,14},{8,0},{10,2},{12,4},{14,6},{1,9},{3,11}... | collective-permute-start | bytes 393224 | tf_op jit(solution)/shard_map/ppermute | solution.py:281
  23.3 14.6 %collective-permute-start.6 = (bf16[2,64,512]{2,1,0:T(8,128)(2,1)S(1)}, bf16[2,64,512]{2,1,0:T(8,128)(2,1)S(1)}, u32[]{:S(2)}, u32[]{:S(2)}) collective-permute-start(bf16[2,64,512]{2,1,0:T(8,128)(2,1)S(1)} %pad_maximum_fusion.6), channel_id=1, source_target_pairs={{0,4},{2,6},{4,8},{6,10},{8,12},{10,14},{12,0},{14,2},{1,5},{3,7},... | collective-permute-start | bytes 393224 | tf_op jit(solution)/shard_map/ppermute | solution.py:281
  23.4 15.2 %collective-permute-start.7 = (bf16[2,64,512]{2,1,0:T(8,128)(2,1)S(1)}, bf16[2,64,512]{2,1,0:T(8,128)(2,1)S(1)}, u32[]{:S(2)}, u32[]{:S(2)}) collective-permute-start(bf16[2,64,512]{2,1,0:T(8,128)(2,1)S(1)} %pad_maximum_fusion.7), channel_id=1, source_target_pairs={{0,12},{2,14},{4,0},{6,2},{8,4},{10,6},{12,8},{14,10},{1,13},{3,15... | collective-permute-start | bytes 393224 | tf_op jit(solution)/shard_map/ppermute | solution.py:281
  38.6 30.5 %copy-start.2 = (bf16[2048,512]{1,0:T(8,128)(2,1)S(1)}, bf16[2048,512]{1,0:T(8,128)(2,1)}, u32[]{:S(2)}) copy-start(bf16[2048,512]{1,0:T(8,128)(2,1)} %down_ref.1) | copy-start | bytes 6291460
  43.8 25.2 %copy-start.1 = (bf16[512,2048]{1,0:T(8,128)(2,1)S(1)}, bf16[512,2048]{1,0:T(8,128)(2,1)}, u32[]{:S(2)}) copy-start(bf16[512,2048]{1,0:T(8,128)(2,1)} %up_ref.1) | copy-start | bytes 6291460

commit v5 on v4

--- a/solution.py
+++ b/solution.py
@@ -46,9 +46,11 @@
     return jnp.where(row == column, 1.0, 0.0).astype(BF16)
 
 
-def attend(x, gain, qkv_ref, out_ref):
+def attend(x, gain, qkv_ref, out_ref, ready=None):
     n = x.shape[0] // LINE
     normed = layer_norm(x, gain)
+    if ready:
+        ready()
     q = (dot(normed, qkv_ref[:, :D]) * (HEAD**-0.5)).astype(BF16)
     k = dot(normed, qkv_ref[:, D : 2 * D]).astype(BF16).T
     v = dot(normed, qkv_ref[:, 2 * D :]).astype(BF16)
@@ -139,10 +141,14 @@
     ]
     for copy in copies:
         copy.start()
-    for copy in copies[:4]:
+    def ready():
+        for copy in copies[2:4]:
+            copy.wait()
+
+    for copy in copies[:2]:
         copy.wait()
     x = x_ref[...].reshape(8 * LINE, D).astype(F32)
-    by_distance(attend(x, gain_ref[0:1, :], qkv_ref, out_ref), y_ref)
+    by_distance(attend(x, gain_ref[0:1, :], qkv_ref, out_ref, ready), y_ref)
     copies[4].wait()
 
 
@@ -216,7 +222,7 @@
 
 def place_kernel(x_ref, y_ref):
     low = lax.broadcasted_iota(jnp.int32, (LINE, D), 0) % 8 < 4
-    for hs in range(8):
+    for hs in range(4):
         first = x_ref[hs // 2, :, hs % 2 * 2].reshape(LINE, D).astype(F32)
         second = x_ref[hs // 2, :, hs % 2 * 2 + 1].reshape(LINE, D).astype(F32)
         y_ref[0, hs] = jnp.where(low, first, pltpu.roll(second, 4, 0)).astype(BF16)
@@ -224,7 +230,7 @@
 
 
 PARAMS = pltpu.CompilerParams(vmem_limit_bytes=40 * 1024 * 1024)
-DISTANCES = (0, 1, 7, 3, 5, 4, 2, 6)
+DISTANCES = (0, 7, 3, 5, 4, 2, 6, 1)
 IN_HBM = pl.BlockSpec(memory_space=pltpu.HBM)
 IN_VMEM = pl.BlockSpec(memory_space=pltpu.VMEM)
 
@@ -305,9 +311,9 @@
     held = lax.all_to_all(sent, ("y", "zh", "zl", "x"), split_axis=0, concat_axis=0, tiled=True)
     return pl.pallas_call(
         place_kernel,
-        grid=(1,),
-        in_specs=[whole(4, 8, 4, 8, D)],
-        out_specs=whole(2, 8, LINE, D),
+        grid=(2,),
+        in_specs=[pl.BlockSpec((2, 8, 4, 8, D), lambda i: (i, 0, 0, 0, 0))],
+        out_specs=pl.BlockSpec((2, 4, LINE, D), lambda i: (0, i, 0, 0)),
         out_shape=jax.ShapeDtypeStruct((2, 8, LINE, D), BF16),
         compiler_params=PARAMS,
         name="place",

time: 120 us -> 119 us (level)
  starting transfers between devices: 19.7 us -> 17.2 us
  waiting for transfers between devices: 11.6 us -> 14.1 us
    ppermute x7, waiting for transfers between devices: 11.6 us -> 14.1 us  [body(): lax.ppermute(blocks[i], ('zh', 'zl'), [(z, (z + i) % 8) for z in range(8)])]
    ppermute x7, starting transfers between devices: 16.3 us -> 13.9 us  [body(): lax.ppermute(blocks[i], ('zh', 'zl'), [(z, (z + i) % 8) for z in range(8)])]
  transfers between devices with their start and end apart: 8 -> 8, of which waited for: 3 -> 5; matrix products, arithmetic and copies ran while one was open for 0% -> 0% of each run, Pallas kernels for 2% -> 2%
where the time goes in v5:
time: 119 us
  blocking collectives  63.5 us (53%)
  Pallas kernels  23.4 us (20%)
  starting transfers between devices  17.2 us (14%)
  waiting for transfers between devices  14.1 us (12%)
    all_to_all x1, blocking collectives, body(): lax.all_to_all(sent, ('y', 'zh', 'zl', 'x'), split_axis=0, concat_axis=0,...  37.9 us
    all_to_all x1, blocking collectives, body(): lax.all_to_all(sent, ('y', 'x', 'c'), split_axis=0, concat_axis=0, tiled=...  25.7 us
    ppermute x7, waiting for transfers between devices, body(): lax.ppermute(blocks[i], ('zh', 'zl'), [(z, (z + i) % 8) for z in range(8)])  14.1 us
    ppermute x7, starting transfers between devices, body(): lax.ppermute(blocks[i], ('zh', 'zl'), [(z, (z + i) % 8) for z in range(8)])  13.9 us
    pallas_call x1, Pallas kernels, body(): pl.pallas_call(depth_kernel, grid=(1,), in_specs=[whole(TOKENS, D)] + wei...  10.4 us
    pallas_call x1, Pallas kernels, body(): pl.pallas_call(height_kernel, grid=(1,), in_specs=[whole(2, LINE, D)] * 8...  5.23 us
    pallas_call x1, Pallas kernels, body(): pl.pallas_call(width_away_kernel, in_specs=[IN_HBM] * 4, out_specs=[IN_VM...  4.04 us
    ppermute x1, starting transfers between devices, body(): away = lax.ppermute(away, 'c', [(0, 1), (1, 0)])  3.32 us
  transfers between devices with their start and end apart: 8, of which 5 were waited for; matrix products, arithmetic and copies ran while one was open for 0% of the time, Pallas kernels for 2%

profile of v5, /device:TPU:1, one launch (start us, length us, event | category | flops | bytes accessed | tf_op | source)
XLA Modules:
  0.0 118.6 jit_solution(18114773869082374459)
XLA Ops:
  0.0 4.0 %width_away.1 = (bf16[8,64,512]{2,1,0:T(8,128)(2,1)S(1)}, bf16[8,64,512]{2,1,0:T(8,128)(2,1)S(1)}, f32[4,512]{1,0:T(4,128)S(1)}, bf16[512,1536]{1,0:T(8,128)(2,1)S(1)}, bf16[512,512]{1,0:T(8,128)(2,1)S(1)}) custom-call(bf16[2,8,64,512]{3,2,1,0:T(8,128)(2,1)} %x_hbm.1, f32[4,512]{1,0:T(4,128)} %gain_ref.1, bf16[3,512,1536]{2,1,0:T(8,128)(2,1)} %qkv_ref.1, ...), custom_call_target="tpu_custom_call" | custom-call | tf_op jit(solution)/shard_map/width_away/pallas_call | solution.py:268
  4.1 3.3 %collective-permute-start = (bf16[8,64,512]{2,1,0:T(8,128)(2,1)S(1)}, bf16[8,64,512]{2,1,0:T(8,128)(2,1)S(1)}, u32[]{:S(2)}, u32[]{:S(2)}) collective-permute-start(bf16[8,64,512]{2,1,0:T(8,128)(2,1)S(1)} %get-tuple-element.14), channel_id=1, source_target_pairs={{0,1},{1,0},{2,3},{3,2},{4,5},{5,4},{6,7},{7,6},{8,9},{9,8},{10,11... | collective-permute-start | bytes 1572872 | tf_op jit(solution)/shard_map/ppermute | solution.py:283
  7.4 0.0 slice-start
  7.4 0.0 slice-start.1
  7.4 2.6 %width_home.1 = bf16[8,64,512]{2,1,0:T(8,128)(2,1)S(1)} custom-call(bf16[8,64,512]{2,1,0:T(8,128)(2,1)S(1)} %get-tuple-element.10.x_ref, f32[4,512]{1,0:T(4,128)S(1)} %get-tuple-element.11.gain_ref, bf16[512,1536]{1,0:T(8,128)(2,1)S(1)} %get-tuple-element.12.qkv_ref, bf16[512,512]{1,0:T(8,128)(2,1)S(1)} %get-tuple-element.13.out_ref), custom_call_target="tpu_custom_call" | custom-call | flops 2100000000 | bytes 1048576 | tf_op jit(solution)/shard_map/width_home/pallas_call | solution.py:255
  10.0 0.0 copy-start
  10.0 0.0 copy-start.3
  10.0 0.0 collective-permute-done
  10.1 3.9 %collective-permute-start.1 = (bf16[2,64,512]{2,1,0:T(8,128)(2,1)S(1)}, bf16[2,64,512]{2,1,0:T(8,128)(2,1)S(1)}, u32[]{:S(2)}, u32[]{:S(2)}) collective-permute-start(bf16[2,64,512]{2,1,0:T(8,128)(2,1)S(1)} %pad_maximum_fusion.1), channel_id=1, source_target_pairs={{0,14},{2,0},{4,2},{6,4},{8,6},{10,8},{12,10},{14,12},{1,15},{3,1}... | collective-permute-start | bytes 393224 | tf_op jit(solution)/shard_map/ppermute | solution.py:287
  14.1 0.1 collective-permute-start.2
  14.2 4.5 %collective-permute-start.3 = (bf16[2,64,512]{2,1,0:T(8,128)(2,1)S(1)}, bf16[2,64,512]{2,1,0:T(8,128)(2,1)S(1)}, u32[]{:S(2)}, u32[]{:S(2)}) collective-permute-start(bf16[2,64,512]{2,1,0:T(8,128)(2,1)S(1)} %pad_maximum_fusion.3), channel_id=1, source_target_pairs={{0,10},{2,12},{4,14},{6,0},{8,2},{10,4},{12,6},{14,8},{1,11},{3,13... | collective-permute-start | bytes 393224 | tf_op jit(solution)/shard_map/ppermute | solution.py:287
  18.7 1.5 %collective-permute-start.4 = (bf16[2,64,512]{2,1,0:T(8,128)(2,1)S(1)}, bf16[2,64,512]{2,1,0:T(8,128)(2,1)S(1)}, u32[]{:S(2)}, u32[]{:S(2)}) collective-permute-start(bf16[2,64,512]{2,1,0:T(8,128)(2,1)S(1)} %pad_maximum_fusion.4), channel_id=1, source_target_pairs={{0,8},{2,10},{4,12},{6,14},{8,0},{10,2},{12,4},{14,6},{1,9},{3,11}... | collective-permute-start | bytes 393224 | tf_op jit(solution)/shard_map/ppermute | solution.py:287
  20.2 1.9 %collective-permute-start.5 = (bf16[2,64,512]{2,1,0:T(8,128)(2,1)S(1)}, bf16[2,64,512]{2,1,0:T(8,128)(2,1)S(1)}, u32[]{:S(2)}, u32[]{:S(2)}) collective-permute-start(bf16[2,64,512]{2,1,0:T(8,128)(2,1)S(1)} %pad_maximum_fusion.5), channel_id=1, source_target_pairs={{0,4},{2,6},{4,8},{6,10},{8,12},{10,14},{12,0},{14,2},{1,5},{3,7},... | collective-permute-start | bytes 393224 | tf_op jit(solution)/shard_map/ppermute | solution.py:287
  22.2 0.0 collective-permute-done.1.refs_1_
  22.2 1.8 %collective-permute-start.6 = (bf16[2,64,512]{2,1,0:T(8,128)(2,1)S(1)}, bf16[2,64,512]{2,1,0:T(8,128)(2,1)S(1)}, u32[]{:S(2)}, u32[]{:S(2)}) collective-permute-start(bf16[2,64,512]{2,1,0:T(8,128)(2,1)S(1)} %pad_maximum_fusion.6), channel_id=1, source_target_pairs={{0,12},{2,14},{4,0},{6,2},{8,4},{10,6},{12,8},{14,10},{1,13},{3,15... | collective-permute-start | bytes 393224 | tf_op jit(solution)/shard_map/ppermute | solution.py:287
  24.0 1.3 %collective-permute-done.2.refs_2_ = bf16[2,64,512]{2,1,0:T(8,128)(2,1)S(1)} collective-permute-done((bf16[2,64,512]{2,1,0:T(8,128)(2,1)S(1)}, bf16[2,64,512]{2,1,0:T(8,128)(2,1)S(1)}, u32[]{:S(2)}, u32[]{:S(2)}) %collective-permute-start.2) | collective-permute-done | bytes 131104 | tf_op jit(solution)/shard_map/ppermute | solution.py:287
  25.3 0.2 collective-permute-start.7
  25.4 0.0 collective-permute-done.3.refs_3_
  25.4 9.7 %collective-permute-done.4.refs_4_ = bf16[2,64,512]{2,1,0:T(8,128)(2,1)S(1)} collective-permute-done((bf16[2,64,512]{2,1,0:T(8,128)(2,1)S(1)}, bf16[2,64,512]{2,1,0:T(8,128)(2,1)S(1)}, u32[]{:S(2)}, u32[]{:S(2)}) %collective-permute-start.4) | collective-permute-done | bytes 131104 | tf_op jit(solution)/shard_map/ppermute | solution.py:287
  35.1 1.3 %collective-permute-done.5.refs_5_ = bf16[2,64,512]{2,1,0:T(8,128)(2,1)S(1)} collective-permute-done((bf16[2,64,512]{2,1,0:T(8,128)(2,1)S(1)}, bf16[2,64,512]{2,1,0:T(8,128)(2,1)S(1)}, u32[]{:S(2)}, u32[]{:S(2)}) %collective-permute-start.5) | collective-permute-done | bytes 131104 | tf_op jit(solution)/shard_map/ppermute | solution.py:287
  36.4 1.2 collective-permute-done.6.refs_6_
  37.6 0.7 collective-permute-done.7.refs_7_
  38.3 0.0 slice-done
  38.3 0.0 slice-done.1
  38.3 0.0 copy-done
  38.3 0.0 copy-done.3
  38.3 0.0 copy-start.2
  38.3 5.2 %height.1 = bf16[1024,512]{1,0:T(8,128)(2,1)S(1)} custom-call(bf16[2,64,512]{2,1,0:T(8,128)(2,1)S(1)} %pad_maximum_fusion.refs_0_, bf16[2,64,512]{2,1,0:T(8,128)(2,1)S(1)} %collective-permute-done.1.refs_1_, bf16[2,64,512]{2,1,0:T(8,128)(2,1)S(1)} %collective-permute-done.2.refs_2_, bf16[2,64,512]{2,1,0:T(8,128)(2,1)S(1)} %collective-permute-done.3.refs_3_, ...), custom_call_target="tpu_custom_call" | custom-call | tf_op jit(solution)/shard_map/height/pallas_call | solution.py:289
  43.5 0.0 copy-start.1
  43.5 25.7 %all_to_all.10 = bf16[32,32,512]{2,1,0:T(8,128)(2,1)S(1)} all-to-all(bf16[32,32,512]{2,1,0:T(8,128)(2,1)S(1)} %bitcast.6), channel_id=1, replica_groups=mesh['y'=4,'x'=4,'zh'=2,'zl'=4,'c'=2] {'y','x','c'}, dimensions={0} | all-to-all | bytes 2097152 | tf_op jit(solution)/shard_map/all_to_all | solution.py:300
  69.2 0.0 copy-done.2
  69.2 0.0 copy-done.1
  69.2 10.4 %depth.1 = bf16[1024,512]{1,0:T(8,128)(2,1)S(1)} custom-call(bf16[1024,512]{1,0:T(8,128)(2,1)S(1)} %bitcast.8, f32[4,512]{1,0:T(4,128)S(1)} %copy-done.3, bf16[3,512,1536]{2,1,0:T(8,128)(2,1)S(1)} %bitcast.5, bf16[3,512,512]{2,1,0:T(8,128)(2,1)S(1)} %copy-done, bf16[512,2048]{1,0:T(8,128)(2,1)S(1)} %copy-done.1, bf16[2048,512]{1,0:T(8,128)(2,1)S(1)} %copy-done.2), custom_call_target="tpu_custom_call" | custom-call | tf_op jit(solution)/shard_map/depth/pallas_call | solution.py:301
  79.6 37.9 %all_to_all.11 = bf16[128,8,512]{2,1,0:T(8,128)(2,1)S(1)} all-to-all(bf16[128,8,512]{2,1,0:T(8,128)(2,1)S(1)} %bitcast.9), channel_id=1, replica_groups=mesh['y'=4,'x'=4,'zh'=2,'zl'=4,'c'=2] {'y','zh','zl','x'}, dimensions={0} | all-to-all | bytes 2097152 | tf_op jit(solution)/shard_map/all_to_all | solution.py:311
  117.4 1.2 place.1
  (11 shorter events, 0.2 us)
Async XLA Ops:
  4.1 6.0 %collective-permute-start = (bf16[8,64,512]{2,1,0:T(8,128)(2,1)S(1)}, bf16[8,64,512]{2,1,0:T(8,128)(2,1)S(1)}, u32[]{:S(2)}, u32[]{:S(2)}) collective-permute-start(bf16[8,64,512]{2,1,0:T(8,128)(2,1)S(1)} %get-tuple-element.14), channel_id=1, source_target_pairs={{0,1},{1,0},{2,3},{3,2},{4,5},{5,4},{6,7},{7,6},{8,9},{9,8},{10,11... | collective-permute-start | bytes 1572872 | tf_op jit(solution)/shard_map/ppermute | solution.py:283
  7.4 30.9 %slice-start = ((s8[4718592]{0:T(1024)(128)(4,1)}), s8[4194304]{0:T(1024)(128)(4,1)S(1)}, s32[]{:S(2)}) async-start(s8[4718592]{0:T(1024)(128)(4,1)} %bitcast.4), calls=%async_computation.2 | async-start | bytes 8388608
  7.4 30.9 %slice-start.1 = ((s8[4718592]{0:T(1024)(128)(4,1)}), s8[524288]{0:T(1024)(128)(4,1)S(1)}, s32[]{:S(2)}) async-start(s8[4718592]{0:T(1024)(128)(4,1)} %bitcast.4), calls=%async_computation.3 | async-start | bytes 1048576
  10.0 28.3 %copy-start = (bf16[3,512,512]{2,1,0:T(8,128)(2,1)S(1)}, bf16[3,512,512]{2,1,0:T(8,128)(2,1)}, u32[]{:S(2)}) copy-start(bf16[3,512,512]{2,1,0:T(8,128)(2,1)} %out_ref.1) | copy-start | bytes 4718596
  10.0 28.3 %copy-start.3 = (f32[4,512]{1,0:T(4,128)S(1)}, f32[4,512]{1,0:T(4,128)}, u32[]{:S(2)}) copy-start(f32[4,512]{1,0:T(4,128)} %gain_ref.1) | copy-start | bytes 24580
  10.1 12.1 %collective-permute-start.1 = (bf16[2,64,512]{2,1,0:T(8,128)(2,1)S(1)}, bf16[2,64,512]{2,1,0:T(8,128)(2,1)S(1)}, u32[]{:S(2)}, u32[]{:S(2)}) collective-permute-start(bf16[2,64,512]{2,1,0:T(8,128)(2,1)S(1)} %pad_maximum_fusion.1), channel_id=1, source_target_pairs={{0,14},{2,0},{4,2},{6,4},{8,6},{10,8},{12,10},{14,12},{1,15},{3,1}... | collective-permute-start | bytes 393224 | tf_op jit(solution)/shard_map/ppermute | solution.py:287
  14.1 11.2 %collective-permute-start.2 = (bf16[2,64,512]{2,1,0:T(8,128)(2,1)S(1)}, bf16[2,64,512]{2,1,0:T(8,128)(2,1)S(1)}, u32[]{:S(2)}, u32[]{:S(2)}) collective-permute-start(bf16[2,64,512]{2,1,0:T(8,128)(2,1)S(1)} %pad_maximum_fusion.2), channel_id=1, source_target_pairs={{0,6},{2,8},{4,10},{6,12},{8,14},{10,0},{12,2},{14,4},{1,7},{3,9},... | collective-permute-start | bytes 393224 | tf_op jit(solution)/shard_map/ppermute | solution.py:287
  14.2 11.3 %collective-permute-start.3 = (bf16[2,64,512]{2,1,0:T(8,128)(2,1)S(1)}, bf16[2,64,512]{2,1,0:T(8,128)(2,1)S(1)}, u32[]{:S(2)}, u32[]{:S(2)}) collective-permute-start(bf16[2,64,512]{2,1,0:T(8,128)(2,1)S(1)} %pad_maximum_fusion.3), channel_id=1, source_target_pairs={{0,10},{2,12},{4,14},{6,0},{8,2},{10,4},{12,6},{14,8},{1,11},{3,13... | collective-permute-start | bytes 393224 | tf_op jit(solution)/shard_map/ppermute | solution.py:287
  18.7 16.4 %collective-permute-start.4 = (bf16[2,64,512]{2,1,0:T(8,128)(2,1)S(1)}, bf16[2,64,512]{2,1,0:T(8,128)(2,1)S(1)}, u32[]{:S(2)}, u32[]{:S(2)}) collective-permute-start(bf16[2,64,512]{2,1,0:T(8,128)(2,1)S(1)} %pad_maximum_fusion.4), channel_id=1, source_target_pairs={{0,8},{2,10},{4,12},{6,14},{8,0},{10,2},{12,4},{14,6},{1,9},{3,11}... | collective-permute-start | bytes 393224 | tf_op jit(solution)/shard_map/ppermute | solution.py:287
  20.2 16.2 %collective-permute-start.5 = (bf16[2,64,512]{2,1,0:T(8,128)(2,1)S(1)}, bf16[2,64,512]{2,1,0:T(8,128)(2,1)S(1)}, u32[]{:S(2)}, u32[]{:S(2)}) collective-permute-start(bf16[2,64,512]{2,1,0:T(8,128)(2,1)S(1)} %pad_maximum_fusion.5), channel_id=1, source_target_pairs={{0,4},{2,6},{4,8},{6,10},{8,12},{10,14},{12,0},{14,2},{1,5},{3,7},... | collective-permute-start | bytes 393224 | tf_op jit(solution)/shard_map/ppermute | solution.py:287
  22.2 15.4 %collective-permute-start.6 = (bf16[2,64,512]{2,1,0:T(8,128)(2,1)S(1)}, bf16[2,64,512]{2,1,0:T(8,128)(2,1)S(1)}, u32[]{:S(2)}, u32[]{:S(2)}) collective-permute-start(bf16[2,64,512]{2,1,0:T(8,128)(2,1)S(1)} %pad_maximum_fusion.6), channel_id=1, source_target_pairs={{0,12},{2,14},{4,0},{6,2},{8,4},{10,6},{12,8},{14,10},{1,13},{3,15... | collective-permute-start | bytes 393224 | tf_op jit(solution)/shard_map/ppermute | solution.py:287
  25.3 13.0 %collective-permute-start.7 = (bf16[2,64,512]{2,1,0:T(8,128)(2,1)S(1)}, bf16[2,64,512]{2,1,0:T(8,128)(2,1)S(1)}, u32[]{:S(2)}, u32[]{:S(2)}) collective-permute-start(bf16[2,64,512]{2,1,0:T(8,128)(2,1)S(1)} %pad_maximum_fusion.7), channel_id=1, source_target_pairs={{0,2},{2,4},{4,6},{6,8},{8,10},{10,12},{12,14},{14,0},{1,3},{3,5},... | collective-permute-start | bytes 393224 | tf_op jit(solution)/shard_map/ppermute | solution.py:287
  38.3 30.9 %copy-start.2 = (bf16[2048,512]{1,0:T(8,128)(2,1)S(1)}, bf16[2048,512]{1,0:T(8,128)(2,1)}, u32[]{:S(2)}) copy-start(bf16[2048,512]{1,0:T(8,128)(2,1)} %down_ref.1) | copy-start | bytes 6291460
  43.5 25.7 %copy-start.1 = (bf16[512,2048]{1,0:T(8,128)(2,1)S(1)}, bf16[512,2048]{1,0:T(8,128)(2,1)}, u32[]{:S(2)}) copy-start(bf16[512,2048]{1,0:T(8,128)(2,1)} %up_ref.1) | copy-start | bytes 6291460

commit v6 on v5

--- a/solution.py
+++ b/solution.py
@@ -185,7 +185,7 @@
             ]
             for hs in range(8):
                 rows = jnp.concatenate([tiles[zl][hs] for zl in range(4)], axis=0)
-                y_ref[pl.ds(hs * 128 + wsub * 64 + c * 32, 32), :] = rows.astype(BF16)
+                y_ref[pl.ds((hs % 2 * 2 + wsub) * 256 + hs // 2 * 64 + c * 32, 32), :] = rows.astype(BF16)
 
 
 def depth_kernel(x_ref, gain_ref, qkv_ref, out_ref, up_ref, down_ref, y_ref):
@@ -194,18 +194,18 @@
     for yh in range(2):
         for d0 in range(2):
             for zl in range(4):
-                tile = [x[((yh * 8 + yl) * 2 + d0) * 32 + zl * 8 :][:8] for yl in range(8)]
+                tile = [x[(yl % 4 * 8 + (yh * 2 + yl // 4) * 2 + d0) * 32 + zl * 8 :][:8] for yl in range(8)]
                 for i, piece in enumerate(turn(tile)):
                     pieces[zl, i % 4, i // 4, d0, yh] = piece
     x = jnp.concatenate([pieces[key] for key in sorted(pieces)], axis=0)
     x = attend(x, gain_ref[2:3, :], qkv_ref, out_ref)
     x = x.astype(BF16).astype(F32)
     normed = layer_norm(x, gain_ref[3:4, :])
-    total = x
-    for part in range(2):
-        cols = slice(part * 1024, (part + 1) * 1024)
-        hidden = jax.nn.gelu(dot(normed, up_ref[:, cols])).astype(BF16)
-        total = total + dot(hidden, down_ref[cols, :])
+    parts = []
+    for at in range(0, TOKENS, 512):
+        hidden = jax.nn.gelu(dot(normed[at : at + 512], up_ref[...])).astype(BF16)
+        parts.append(x[at : at + 512] + dot(hidden, down_ref[...]))
+    total = jnp.concatenate(parts, axis=0)
     pieces = {key: total[8 * i : 8 * i + 8] for i, key in enumerate(sorted(pieces))}
     for zh in range(2):
         for yh in range(2):
@@ -297,7 +297,7 @@
         name="height",
     )(*held, *weights)
     sent = sent.reshape(32, 32, D)
-    held = lax.all_to_all(sent, ("y", "x", "c"), split_axis=0, concat_axis=0, tiled=True)
+    held = lax.all_to_all(sent, ("x", "y", "c"), split_axis=0, concat_axis=0, tiled=True)
     sent = pl.pallas_call(
         depth_kernel,
         grid=(1,),

time: 119 us -> 118 us (level)
  blocking collectives: 63.5 us -> 61.8 us
    all_to_all x1, blocking collectives: 37.9 us -> 36.4 us  [body(): lax.all_to_all(sent, ('y', 'zh', 'zl', 'x'), split_axis=0, concat_axis=0,...]
where the time goes in v6:
time: 118 us; the launch traced here: 117 us
  blocking collectives  61.8 us (52%)
  Pallas kernels  23.2 us (20%)
  starting transfers between devices  17.2 us (15%)
  waiting for transfers between devices  14.1 us (12%)
    all_to_all x1, blocking collectives, body(): lax.all_to_all(sent, ('y', 'zh', 'zl', 'x'), split_axis=0, concat_axis=0,...  36.4 us
    all_to_all x1, blocking collectives, body(): lax.all_to_all(sent, ('x', 'y', 'c'), split_axis=0, concat_axis=0, tiled=...  25.4 us
    ppermute x7, waiting for transfers between devices, body(): lax.ppermute(blocks[i], ('zh', 'zl'), [(z, (z + i) % 8) for z in range(8)])  14.1 us
    ppermute x7, starting transfers between devices, body(): lax.ppermute(blocks[i], ('zh', 'zl'), [(z, (z + i) % 8) for z in range(8)])  13.9 us
    pallas_call x1, Pallas kernels, body(): pl.pallas_call(depth_kernel, grid=(1,), in_specs=[whole(TOKENS, D)] + wei...  10.2 us
    pallas_call x1, Pallas kernels, body(): pl.pallas_call(height_kernel, grid=(1,), in_specs=[whole(2, LINE, D)] * 8...  5.23 us
    pallas_call x1, Pallas kernels, body(): pl.pallas_call(width_away_kernel, in_specs=[IN_HBM] * 4, out_specs=[IN_VM...  4.04 us
    ppermute x1, starting transfers between devices, body(): away = lax.ppermute(away, 'c', [(0, 1), (1, 0)])  3.32 us
  transfers between devices with their start and end apart: 8, of which 5 were waited for; matrix products, arithmetic and copies ran while one was open for 0% of the time, Pallas kernels for 2%

profile of v6, /device:TPU:1, one launch (start us, length us, event | category | flops | bytes accessed | tf_op | source)
XLA Modules:
  0.0 116.7 jit_solution(2958471647243863248)
XLA Ops:
  0.0 4.0 %width_away.1 = (bf16[8,64,512]{2,1,0:T(8,128)(2,1)S(1)}, bf16[8,64,512]{2,1,0:T(8,128)(2,1)S(1)}, f32[4,512]{1,0:T(4,128)S(1)}, bf16[512,1536]{1,0:T(8,128)(2,1)S(1)}, bf16[512,512]{1,0:T(8,128)(2,1)S(1)}) custom-call(bf16[2,8,64,512]{3,2,1,0:T(8,128)(2,1)} %x_hbm.1, f32[4,512]{1,0:T(4,128)} %gain_ref.1, bf16[3,512,1536]{2,1,0:T(8,128)(2,1)} %qkv_ref.1, ...), custom_call_target="tpu_custom_call" | custom-call | tf_op jit(solution)/shard_map/width_away/pallas_call | solution.py:268
  4.1 3.3 %collective-permute-start = (bf16[8,64,512]{2,1,0:T(8,128)(2,1)S(1)}, bf16[8,64,512]{2,1,0:T(8,128)(2,1)S(1)}, u32[]{:S(2)}, u32[]{:S(2)}) collective-permute-start(bf16[8,64,512]{2,1,0:T(8,128)(2,1)S(1)} %get-tuple-element.14), channel_id=1, source_target_pairs={{0,1},{1,0},{2,3},{3,2},{4,5},{5,4},{6,7},{7,6},{8,9},{9,8},{10,11... | collective-permute-start | bytes 1572872 | tf_op jit(solution)/shard_map/ppermute | solution.py:283
  7.4 0.0 slice-start
  7.4 0.0 slice-start.1
  7.4 2.6 %width_home.1 = bf16[8,64,512]{2,1,0:T(8,128)(2,1)S(1)} custom-call(bf16[8,64,512]{2,1,0:T(8,128)(2,1)S(1)} %get-tuple-element.10.x_ref, f32[4,512]{1,0:T(4,128)S(1)} %get-tuple-element.11.gain_ref, bf16[512,1536]{1,0:T(8,128)(2,1)S(1)} %get-tuple-element.12.qkv_ref, bf16[512,512]{1,0:T(8,128)(2,1)S(1)} %get-tuple-element.13.out_ref), custom_call_target="tpu_custom_call" | custom-call | flops 2100000000 | bytes 1048576 | tf_op jit(solution)/shard_map/width_home/pallas_call | solution.py:255
  10.0 0.0 copy-start
  10.0 0.0 copy-start.3
  10.0 0.0 collective-permute-done
  10.1 3.9 %collective-permute-start.1 = (bf16[2,64,512]{2,1,0:T(8,128)(2,1)S(1)}, bf16[2,64,512]{2,1,0:T(8,128)(2,1)S(1)}, u32[]{:S(2)}, u32[]{:S(2)}) collective-permute-start(bf16[2,64,512]{2,1,0:T(8,128)(2,1)S(1)} %pad_maximum_fusion.1), channel_id=1, source_target_pairs={{0,14},{2,0},{4,2},{6,4},{8,6},{10,8},{12,10},{14,12},{1,15},{3,1}... | collective-permute-start | bytes 393224 | tf_op jit(solution)/shard_map/ppermute | solution.py:287
  14.1 0.1 collective-permute-start.2
  14.2 4.5 %collective-permute-start.3 = (bf16[2,64,512]{2,1,0:T(8,128)(2,1)S(1)}, bf16[2,64,512]{2,1,0:T(8,128)(2,1)S(1)}, u32[]{:S(2)}, u32[]{:S(2)}) collective-permute-start(bf16[2,64,512]{2,1,0:T(8,128)(2,1)S(1)} %pad_maximum_fusion.3), channel_id=1, source_target_pairs={{0,10},{2,12},{4,14},{6,0},{8,2},{10,4},{12,6},{14,8},{1,11},{3,13... | collective-permute-start | bytes 393224 | tf_op jit(solution)/shard_map/ppermute | solution.py:287
  18.7 1.5 %collective-permute-start.4 = (bf16[2,64,512]{2,1,0:T(8,128)(2,1)S(1)}, bf16[2,64,512]{2,1,0:T(8,128)(2,1)S(1)}, u32[]{:S(2)}, u32[]{:S(2)}) collective-permute-start(bf16[2,64,512]{2,1,0:T(8,128)(2,1)S(1)} %pad_maximum_fusion.4), channel_id=1, source_target_pairs={{0,8},{2,10},{4,12},{6,14},{8,0},{10,2},{12,4},{14,6},{1,9},{3,11}... | collective-permute-start | bytes 393224 | tf_op jit(solution)/shard_map/ppermute | solution.py:287
  20.2 1.9 %collective-permute-start.5 = (bf16[2,64,512]{2,1,0:T(8,128)(2,1)S(1)}, bf16[2,64,512]{2,1,0:T(8,128)(2,1)S(1)}, u32[]{:S(2)}, u32[]{:S(2)}) collective-permute-start(bf16[2,64,512]{2,1,0:T(8,128)(2,1)S(1)} %pad_maximum_fusion.5), channel_id=1, source_target_pairs={{0,4},{2,6},{4,8},{6,10},{8,12},{10,14},{12,0},{14,2},{1,5},{3,7},... | collective-permute-start | bytes 393224 | tf_op jit(solution)/shard_map/ppermute | solution.py:287
  22.2 0.0 collective-permute-done.1.refs_1_
  22.2 1.8 %collective-permute-start.6 = (bf16[2,64,512]{2,1,0:T(8,128)(2,1)S(1)}, bf16[2,64,512]{2,1,0:T(8,128)(2,1)S(1)}, u32[]{:S(2)}, u32[]{:S(2)}) collective-permute-start(bf16[2,64,512]{2,1,0:T(8,128)(2,1)S(1)} %pad_maximum_fusion.6), channel_id=1, source_target_pairs={{0,12},{2,14},{4,0},{6,2},{8,4},{10,6},{12,8},{14,10},{1,13},{3,15... | collective-permute-start | bytes 393224 | tf_op jit(solution)/shard_map/ppermute | solution.py:287
  24.0 1.3 %collective-permute-done.2.refs_2_ = bf16[2,64,512]{2,1,0:T(8,128)(2,1)S(1)} collective-permute-done((bf16[2,64,512]{2,1,0:T(8,128)(2,1)S(1)}, bf16[2,64,512]{2,1,0:T(8,128)(2,1)S(1)}, u32[]{:S(2)}, u32[]{:S(2)}) %collective-permute-start.2) | collective-permute-done | bytes 131104 | tf_op jit(solution)/shard_map/ppermute | solution.py:287
  25.3 0.2 collective-permute-start.7
  25.4 0.0 collective-permute-done.3.refs_3_
  25.4 9.7 %collective-permute-done.4.refs_4_ = bf16[2,64,512]{2,1,0:T(8,128)(2,1)S(1)} collective-permute-done((bf16[2,64,512]{2,1,0:T(8,128)(2,1)S(1)}, bf16[2,64,512]{2,1,0:T(8,128)(2,1)S(1)}, u32[]{:S(2)}, u32[]{:S(2)}) %collective-permute-start.4) | collective-permute-done | bytes 131104 | tf_op jit(solution)/shard_map/ppermute | solution.py:287
  35.1 1.3 %collective-permute-done.5.refs_5_ = bf16[2,64,512]{2,1,0:T(8,128)(2,1)S(1)} collective-permute-done((bf16[2,64,512]{2,1,0:T(8,128)(2,1)S(1)}, bf16[2,64,512]{2,1,0:T(8,128)(2,1)S(1)}, u32[]{:S(2)}, u32[]{:S(2)}) %collective-permute-start.5) | collective-permute-done | bytes 131104 | tf_op jit(solution)/shard_map/ppermute | solution.py:287
  36.4 1.2 collective-permute-done.6.refs_6_
  37.6 0.7 collective-permute-done.7.refs_7_
  38.3 0.0 slice-done
  38.3 0.0 slice-done.1
  38.3 0.0 copy-done
  38.3 0.0 copy-done.3
  38.3 0.0 copy-start.2
  38.3 5.2 %height.1 = bf16[1024,512]{1,0:T(8,128)(2,1)S(1)} custom-call(bf16[2,64,512]{2,1,0:T(8,128)(2,1)S(1)} %pad_maximum_fusion.refs_0_, bf16[2,64,512]{2,1,0:T(8,128)(2,1)S(1)} %collective-permute-done.1.refs_1_, bf16[2,64,512]{2,1,0:T(8,128)(2,1)S(1)} %collective-permute-done.2.refs_2_, bf16[2,64,512]{2,1,0:T(8,128)(2,1)S(1)} %collective-permute-done.3.refs_3_, ...), custom_call_target="tpu_custom_call" | custom-call | tf_op jit(solution)/shard_map/height/pallas_call | solution.py:289
  43.5 0.0 copy-start.1
  43.5 25.4 %all_to_all.10 = bf16[32,32,512]{2,1,0:T(8,128)(2,1)S(1)} all-to-all(bf16[32,32,512]{2,1,0:T(8,128)(2,1)S(1)} %bitcast.6), channel_id=1, replica_groups=mesh['y'=4,'x'=4,'zh'=2,'zl'=4,'c'=2] {'x','y','c'}, dimensions={0} | all-to-all | bytes 2097152 | tf_op jit(solution)/shard_map/all_to_all | solution.py:300
  68.9 0.0 copy-done.2
  69.0 0.0 copy-done.1
  69.0 10.2 %depth.1 = bf16[1024,512]{1,0:T(8,128)(2,1)S(1)} custom-call(bf16[1024,512]{1,0:T(8,128)(2,1)S(1)} %bitcast.8, f32[4,512]{1,0:T(4,128)S(1)} %copy-done.3, bf16[3,512,1536]{2,1,0:T(8,128)(2,1)S(1)} %bitcast.5, bf16[3,512,512]{2,1,0:T(8,128)(2,1)S(1)} %copy-done, bf16[512,2048]{1,0:T(8,128)(2,1)S(1)} %copy-done.1, bf16[2048,512]{1,0:T(8,128)(2,1)S(1)} %copy-done.2), custom_call_target="tpu_custom_call" | custom-call | tf_op jit(solution)/shard_map/depth/pallas_call | solution.py:301
  79.2 36.4 %all_to_all.11 = bf16[128,8,512]{2,1,0:T(8,128)(2,1)S(1)} all-to-all(bf16[128,8,512]{2,1,0:T(8,128)(2,1)S(1)} %bitcast.9), channel_id=1, replica_groups=mesh['y'=4,'x'=4,'zh'=2,'zl'=4,'c'=2] {'y','zh','zl','x'}, dimensions={0} | all-to-all | bytes 2097152 | tf_op jit(solution)/shard_map/all_to_all | solution.py:311
  115.5 1.2 place.1
  (11 shorter events, 0.2 us)
Async XLA Ops:
  4.1 6.0 %collective-permute-start = (bf16[8,64,512]{2,1,0:T(8,128)(2,1)S(1)}, bf16[8,64,512]{2,1,0:T(8,128)(2,1)S(1)}, u32[]{:S(2)}, u32[]{:S(2)}) collective-permute-start(bf16[8,64,512]{2,1,0:T(8,128)(2,1)S(1)} %get-tuple-element.14), channel_id=1, source_target_pairs={{0,1},{1,0},{2,3},{3,2},{4,5},{5,4},{6,7},{7,6},{8,9},{9,8},{10,11... | collective-permute-start | bytes 1572872 | tf_op jit(solution)/shard_map/ppermute | solution.py:283
  7.4 30.9 %slice-start = ((s8[4718592]{0:T(1024)(128)(4,1)}), s8[4194304]{0:T(1024)(128)(4,1)S(1)}, s32[]{:S(2)}) async-start(s8[4718592]{0:T(1024)(128)(4,1)} %bitcast.4), calls=%async_computation.2 | async-start | bytes 8388608
  7.4 30.9 %slice-start.1 = ((s8[4718592]{0:T(1024)(128)(4,1)}), s8[524288]{0:T(1024)(128)(4,1)S(1)}, s32[]{:S(2)}) async-start(s8[4718592]{0:T(1024)(128)(4,1)} %bitcast.4), calls=%async_computation.3 | async-start | bytes 1048576
  10.0 28.3 %copy-start = (bf16[3,512,512]{2,1,0:T(8,128)(2,1)S(1)}, bf16[3,512,512]{2,1,0:T(8,128)(2,1)}, u32[]{:S(2)}) copy-start(bf16[3,512,512]{2,1,0:T(8,128)(2,1)} %out_ref.1) | copy-start | bytes 4718596
  10.0 28.3 %copy-start.3 = (f32[4,512]{1,0:T(4,128)S(1)}, f32[4,512]{1,0:T(4,128)}, u32[]{:S(2)}) copy-start(f32[4,512]{1,0:T(4,128)} %gain_ref.1) | copy-start | bytes 24580
  10.1 12.1 %collective-permute-start.1 = (bf16[2,64,512]{2,1,0:T(8,128)(2,1)S(1)}, bf16[2,64,512]{2,1,0:T(8,128)(2,1)S(1)}, u32[]{:S(2)}, u32[]{:S(2)}) collective-permute-start(bf16[2,64,512]{2,1,0:T(8,128)(2,1)S(1)} %pad_maximum_fusion.1), channel_id=1, source_target_pairs={{0,14},{2,0},{4,2},{6,4},{8,6},{10,8},{12,10},{14,12},{1,15},{3,1}... | collective-permute-start | bytes 393224 | tf_op jit(solution)/shard_map/ppermute | solution.py:287
  14.1 11.2 %collective-permute-start.2 = (bf16[2,64,512]{2,1,0:T(8,128)(2,1)S(1)}, bf16[2,64,512]{2,1,0:T(8,128)(2,1)S(1)}, u32[]{:S(2)}, u32[]{:S(2)}) collective-permute-start(bf16[2,64,512]{2,1,0:T(8,128)(2,1)S(1)} %pad_maximum_fusion.2), channel_id=1, source_target_pairs={{0,6},{2,8},{4,10},{6,12},{8,14},{10,0},{12,2},{14,4},{1,7},{3,9},... | collective-permute-start | bytes 393224 | tf_op jit(solution)/shard_map/ppermute | solution.py:287
  14.2 11.3 %collective-permute-start.3 = (bf16[2,64,512]{2,1,0:T(8,128)(2,1)S(1)}, bf16[2,64,512]{2,1,0:T(8,128)(2,1)S(1)}, u32[]{:S(2)}, u32[]{:S(2)}) collective-permute-start(bf16[2,64,512]{2,1,0:T(8,128)(2,1)S(1)} %pad_maximum_fusion.3), channel_id=1, source_target_pairs={{0,10},{2,12},{4,14},{6,0},{8,2},{10,4},{12,6},{14,8},{1,11},{3,13... | collective-permute-start | bytes 393224 | tf_op jit(solution)/shard_map/ppermute | solution.py:287
  18.7 16.4 %collective-permute-start.4 = (bf16[2,64,512]{2,1,0:T(8,128)(2,1)S(1)}, bf16[2,64,512]{2,1,0:T(8,128)(2,1)S(1)}, u32[]{:S(2)}, u32[]{:S(2)}) collective-permute-start(bf16[2,64,512]{2,1,0:T(8,128)(2,1)S(1)} %pad_maximum_fusion.4), channel_id=1, source_target_pairs={{0,8},{2,10},{4,12},{6,14},{8,0},{10,2},{12,4},{14,6},{1,9},{3,11}... | collective-permute-start | bytes 393224 | tf_op jit(solution)/shard_map/ppermute | solution.py:287
  20.2 16.2 %collective-permute-start.5 = (bf16[2,64,512]{2,1,0:T(8,128)(2,1)S(1)}, bf16[2,64,512]{2,1,0:T(8,128)(2,1)S(1)}, u32[]{:S(2)}, u32[]{:S(2)}) collective-permute-start(bf16[2,64,512]{2,1,0:T(8,128)(2,1)S(1)} %pad_maximum_fusion.5), channel_id=1, source_target_pairs={{0,4},{2,6},{4,8},{6,10},{8,12},{10,14},{12,0},{14,2},{1,5},{3,7},... | collective-permute-start | bytes 393224 | tf_op jit(solution)/shard_map/ppermute | solution.py:287
  22.2 15.4 %collective-permute-start.6 = (bf16[2,64,512]{2,1,0:T(8,128)(2,1)S(1)}, bf16[2,64,512]{2,1,0:T(8,128)(2,1)S(1)}, u32[]{:S(2)}, u32[]{:S(2)}) collective-permute-start(bf16[2,64,512]{2,1,0:T(8,128)(2,1)S(1)} %pad_maximum_fusion.6), channel_id=1, source_target_pairs={{0,12},{2,14},{4,0},{6,2},{8,4},{10,6},{12,8},{14,10},{1,13},{3,15... | collective-permute-start | bytes 393224 | tf_op jit(solution)/shard_map/ppermute | solution.py:287
  25.3 13.0 %collective-permute-start.7 = (bf16[2,64,512]{2,1,0:T(8,128)(2,1)S(1)}, bf16[2,64,512]{2,1,0:T(8,128)(2,1)S(1)}, u32[]{:S(2)}, u32[]{:S(2)}) collective-permute-start(bf16[2,64,512]{2,1,0:T(8,128)(2,1)S(1)} %pad_maximum_fusion.7), channel_id=1, source_target_pairs={{0,2},{2,4},{4,6},{6,8},{8,10},{10,12},{12,14},{14,0},{1,3},{3,5},... | collective-permute-start | bytes 393224 | tf_op jit(solution)/shard_map/ppermute | solution.py:287
  38.3 30.7 %copy-start.2 = (bf16[2048,512]{1,0:T(8,128)(2,1)S(1)}, bf16[2048,512]{1,0:T(8,128)(2,1)}, u32[]{:S(2)}) copy-start(bf16[2048,512]{1,0:T(8,128)(2,1)} %down_ref.1) | copy-start | bytes 6291460
  43.5 25.4 %copy-start.1 = (bf16[512,2048]{1,0:T(8,128)(2,1)S(1)}, bf16[512,2048]{1,0:T(8,128)(2,1)}, u32[]{:S(2)}) copy-start(bf16[512,2048]{1,0:T(8,128)(2,1)} %up_ref.1) | copy-start | bytes 6291460

commit v7 on v6

--- a/solution.py
+++ b/solution.py
@@ -216,21 +216,29 @@
             for y in range(2):
                 for zl in range(4):
                     rows = jnp.concatenate(tiles[zl][4 * y : 4 * y + 4], axis=0)
-                    at = ((yh * 2 + y) * 8 + zh * 4 + zl) * 32
+                    at = ((yh * 2 + y) * 8 + Z_PLACE[zh * 4 + zl]) * 32
                     y_ref[pl.ds(at, 32), :] = rows.astype(BF16)
 
 
 def place_kernel(x_ref, y_ref):
     low = lax.broadcasted_iota(jnp.int32, (LINE, D), 0) % 8 < 4
     for hs in range(4):
-        first = x_ref[hs // 2, :, hs % 2 * 2].reshape(LINE, D).astype(F32)
-        second = x_ref[hs // 2, :, hs % 2 * 2 + 1].reshape(LINE, D).astype(F32)
+        first, second = [
+            jnp.concatenate(
+                [x_ref[hs // 2, place, hs % 2 * 2 + wsub].astype(F32) for place in Z_PLACE], axis=0
+            )
+            for wsub in range(2)
+        ]
         y_ref[0, hs] = jnp.where(low, first, pltpu.roll(second, 4, 0)).astype(BF16)
         y_ref[1, hs] = jnp.where(low, pltpu.roll(first, LINE - 4, 0), second).astype(BF16)
 
 
 PARAMS = pltpu.CompilerParams(vmem_limit_bytes=40 * 1024 * 1024)
-DISTANCES = (0, 7, 3, 5, 4, 2, 6, 1)
+Z_PLACE = [3 * z % 8 for z in range(8)]
+GROUPS = [
+    [((y * 4 + x) * 8 + z) * 2 + core for y in range(4) for z in Z_PLACE for x in range(4)] for core in range(2)
+]
+DISTANCES = (0, 1, 5, 3, 4, 6, 2, 7)
 IN_HBM = pl.BlockSpec(memory_space=pltpu.HBM)
 IN_VMEM = pl.BlockSpec(memory_space=pltpu.VMEM)
 
@@ -308,7 +316,9 @@
         name="depth",
     )(held.reshape(TOKENS, D), *weights, up_weight, down_weight)
     sent = sent.reshape(128, 8, D)
-    held = lax.all_to_all(sent, ("y", "zh", "zl", "x"), split_axis=0, concat_axis=0, tiled=True)
+    held = lax.all_to_all(
+        sent, ("y", "x", "zh", "zl", "c"), split_axis=0, concat_axis=0, tiled=True, axis_index_groups=GROUPS
+    )
     return pl.pallas_call(
         place_kernel,
         grid=(2,),

time: 118 us -> 117 us (level); the launches traced: 117 us -> 117 us
  starting transfers between devices: 17.2 us -> 20.2 us
  blocking collectives: 61.8 us -> 60.1 us
    ppermute x7, starting transfers between devices: 13.9 us -> 16.9 us  [body(): lax.ppermute(blocks[i], ('zh', 'zl'), [(z, (z + i) % 8) for z in range(8)])]
  transfers between devices with their start and end apart: 8 -> 8, of which waited for: 5 -> 4; matrix products, arithmetic and copies ran while one was open for 0% -> 0% of each run, Pallas kernels for 2% -> 2%
where the time goes in v7:
time: 117 us
  blocking collectives  60.1 us (51%)
  Pallas kernels  23.2 us (20%)
  starting transfers between devices  20.2 us (17%)
  waiting for transfers between devices  13.2 us (11%)
    all_to_all x1, blocking collectives, body(): lax.all_to_all(sent, ('y', 'x', 'zh', 'zl', 'c'), split_axis=0, concat_ax...  35.6 us
    all_to_all x1, blocking collectives, body(): lax.all_to_all(sent, ('x', 'y', 'c'), split_axis=0, concat_axis=0, tiled=...  24.4 us
    ppermute x7, starting transfers between devices, body(): lax.ppermute(blocks[i], ('zh', 'zl'), [(z, (z + i) % 8) for z in range(8)])  16.9 us
    ppermute x7, waiting for transfers between devices, body(): lax.ppermute(blocks[i], ('zh', 'zl'), [(z, (z + i) % 8) for z in range(8)])  13.2 us
    pallas_call x1, Pallas kernels, body(): pl.pallas_call(depth_kernel, grid=(1,), in_specs=[whole(TOKENS, D)] + wei...  10.2 us
    pallas_call x1, Pallas kernels, body(): pl.pallas_call(height_kernel, grid=(1,), in_specs=[whole(2, LINE, D)] * 8...  5.22 us
    pallas_call x1, Pallas kernels, body(): pl.pallas_call(width_away_kernel, in_specs=[IN_HBM] * 4, out_specs=[IN_VM...  4.04 us
    ppermute x1, starting transfers between devices, body(): away = lax.ppermute(away, 'c', [(0, 1), (1, 0)])  3.32 us
  transfers between devices with their start and end apart: 8, of which 4 were waited for; matrix products, arithmetic and copies ran while one was open for 0% of the time, Pallas kernels for 2%

profile of v7, /device:TPU:1, one launch (start us, length us, event | category | flops | bytes accessed | tf_op | source)
XLA Modules:
  0.0 117.1 jit_solution(18327837766338793432)
XLA Ops:
  0.0 4.0 %width_away.1 = (bf16[8,64,512]{2,1,0:T(8,128)(2,1)S(1)}, bf16[8,64,512]{2,1,0:T(8,128)(2,1)S(1)}, f32[4,512]{1,0:T(4,128)S(1)}, bf16[512,1536]{1,0:T(8,128)(2,1)S(1)}, bf16[512,512]{1,0:T(8,128)(2,1)S(1)}) custom-call(bf16[2,8,64,512]{3,2,1,0:T(8,128)(2,1)} %x_hbm.1, f32[4,512]{1,0:T(4,128)} %gain_ref.1, bf16[3,512,1536]{2,1,0:T(8,128)(2,1)} %qkv_ref.1, ...), custom_call_target="tpu_custom_call" | custom-call | tf_op jit(solution)/shard_map/width_away/pallas_call | solution.py:276
  4.1 3.3 %collective-permute-start = (bf16[8,64,512]{2,1,0:T(8,128)(2,1)S(1)}, bf16[8,64,512]{2,1,0:T(8,128)(2,1)S(1)}, u32[]{:S(2)}, u32[]{:S(2)}) collective-permute-start(bf16[8,64,512]{2,1,0:T(8,128)(2,1)S(1)} %get-tuple-element.14), channel_id=1, source_target_pairs={{0,1},{1,0},{2,3},{3,2},{4,5},{5,4},{6,7},{7,6},{8,9},{9,8},{10,11... | collective-permute-start | bytes 1572872 | tf_op jit(solution)/shard_map/ppermute | solution.py:291
  7.4 0.0 slice-start
  7.4 0.0 slice-start.1
  7.4 2.6 %width_home.1 = bf16[8,64,512]{2,1,0:T(8,128)(2,1)S(1)} custom-call(bf16[8,64,512]{2,1,0:T(8,128)(2,1)S(1)} %get-tuple-element.10.x_ref, f32[4,512]{1,0:T(4,128)S(1)} %get-tuple-element.11.gain_ref, bf16[512,1536]{1,0:T(8,128)(2,1)S(1)} %get-tuple-element.12.qkv_ref, bf16[512,512]{1,0:T(8,128)(2,1)S(1)} %get-tuple-element.13.out_ref), custom_call_target="tpu_custom_call" | custom-call | flops 2100000000 | bytes 1048576 | tf_op jit(solution)/shard_map/width_home/pallas_call | solution.py:263
  10.0 0.0 copy-start
  10.0 0.0 copy-start.3
  10.0 0.0 collective-permute-done
  10.1 0.1 collective-permute-start.1
  10.2 5.5 %collective-permute-start.2 = (bf16[2,64,512]{2,1,0:T(8,128)(2,1)S(1)}, bf16[2,64,512]{2,1,0:T(8,128)(2,1)S(1)}, u32[]{:S(2)}, u32[]{:S(2)}) collective-permute-start(bf16[2,64,512]{2,1,0:T(8,128)(2,1)S(1)} %pad_maximum_fusion.2), channel_id=1, source_target_pairs={{0,10},{2,12},{4,14},{6,0},{8,2},{10,4},{12,6},{14,8},{1,11},{3,13... | collective-permute-start | bytes 393224 | tf_op jit(solution)/shard_map/ppermute | solution.py:295
  15.8 0.1 collective-permute-start.3
  15.9 3.8 %collective-permute-start.4 = (bf16[2,64,512]{2,1,0:T(8,128)(2,1)S(1)}, bf16[2,64,512]{2,1,0:T(8,128)(2,1)S(1)}, u32[]{:S(2)}, u32[]{:S(2)}) collective-permute-start(bf16[2,64,512]{2,1,0:T(8,128)(2,1)S(1)} %pad_maximum_fusion.4), channel_id=1, source_target_pairs={{0,8},{2,10},{4,12},{6,14},{8,0},{10,2},{12,4},{14,6},{1,9},{3,11}... | collective-permute-start | bytes 393224 | tf_op jit(solution)/shard_map/ppermute | solution.py:295
  19.7 1.6 %collective-permute-start.5 = (bf16[2,64,512]{2,1,0:T(8,128)(2,1)S(1)}, bf16[2,64,512]{2,1,0:T(8,128)(2,1)S(1)}, u32[]{:S(2)}, u32[]{:S(2)}) collective-permute-start(bf16[2,64,512]{2,1,0:T(8,128)(2,1)S(1)} %pad_maximum_fusion.5), channel_id=1, source_target_pairs={{0,12},{2,14},{4,0},{6,2},{8,4},{10,6},{12,8},{14,10},{1,13},{3,15... | collective-permute-start | bytes 393224 | tf_op jit(solution)/shard_map/ppermute | solution.py:295
  21.3 0.0 collective-permute-done.1.refs_1_
  21.3 1.0 collective-permute-start.6
  22.3 2.4 %collective-permute-done.2.refs_2_ = bf16[2,64,512]{2,1,0:T(8,128)(2,1)S(1)} collective-permute-done((bf16[2,64,512]{2,1,0:T(8,128)(2,1)S(1)}, bf16[2,64,512]{2,1,0:T(8,128)(2,1)S(1)}, u32[]{:S(2)}, u32[]{:S(2)}) %collective-permute-start.2) | collective-permute-done | bytes 131104 | tf_op jit(solution)/shard_map/ppermute | solution.py:295
  24.7 4.9 %collective-permute-start.7 = (bf16[2,64,512]{2,1,0:T(8,128)(2,1)S(1)}, bf16[2,64,512]{2,1,0:T(8,128)(2,1)S(1)}, u32[]{:S(2)}, u32[]{:S(2)}) collective-permute-start(bf16[2,64,512]{2,1,0:T(8,128)(2,1)S(1)} %pad_maximum_fusion.7), channel_id=1, source_target_pairs={{0,14},{2,0},{4,2},{6,4},{8,6},{10,8},{12,10},{14,12},{1,15},{3,1}... | collective-permute-start | bytes 393224 | tf_op jit(solution)/shard_map/ppermute | solution.py:295
  29.6 0.0 collective-permute-done.3.refs_3_
  29.6 0.3 collective-permute-done.4.refs_4_
  29.9 6.9 %collective-permute-done.5.refs_5_ = bf16[2,64,512]{2,1,0:T(8,128)(2,1)S(1)} collective-permute-done((bf16[2,64,512]{2,1,0:T(8,128)(2,1)S(1)}, bf16[2,64,512]{2,1,0:T(8,128)(2,1)S(1)}, u32[]{:S(2)}, u32[]{:S(2)}) %collective-permute-start.5) | collective-permute-done | bytes 131104 | tf_op jit(solution)/shard_map/ppermute | solution.py:295
  36.7 3.7 %collective-permute-done.6.refs_6_ = bf16[2,64,512]{2,1,0:T(8,128)(2,1)S(1)} collective-permute-done((bf16[2,64,512]{2,1,0:T(8,128)(2,1)S(1)}, bf16[2,64,512]{2,1,0:T(8,128)(2,1)S(1)}, u32[]{:S(2)}, u32[]{:S(2)}) %collective-permute-start.6) | collective-permute-done | bytes 131104 | tf_op jit(solution)/shard_map/ppermute | solution.py:295
  40.4 0.0 collective-permute-done.7.refs_7_
  40.4 0.0 slice-done
  40.4 0.0 slice-done.1
  40.4 0.0 copy-done
  40.4 0.0 copy-done.3
  40.4 0.0 copy-start.2
  40.4 5.2 %height.1 = bf16[1024,512]{1,0:T(8,128)(2,1)S(1)} custom-call(bf16[2,64,512]{2,1,0:T(8,128)(2,1)S(1)} %pad_maximum_fusion.refs_0_, bf16[2,64,512]{2,1,0:T(8,128)(2,1)S(1)} %collective-permute-done.1.refs_1_, bf16[2,64,512]{2,1,0:T(8,128)(2,1)S(1)} %collective-permute-done.2.refs_2_, bf16[2,64,512]{2,1,0:T(8,128)(2,1)S(1)} %collective-permute-done.3.refs_3_, ...), custom_call_target="tpu_custom_call" | custom-call | tf_op jit(solution)/shard_map/height/pallas_call | solution.py:297
  45.7 0.0 copy-start.1
  45.7 24.4 %all_to_all.10 = bf16[32,32,512]{2,1,0:T(8,128)(2,1)S(1)} all-to-all(bf16[32,32,512]{2,1,0:T(8,128)(2,1)S(1)} %bitcast.6), channel_id=1, replica_groups=mesh['y'=4,'x'=4,'zh'=2,'zl'=4,'c'=2] {'x','y','c'}, dimensions={0} | all-to-all | bytes 2097152 | tf_op jit(solution)/shard_map/all_to_all | solution.py:308
  70.1 0.0 copy-done.2
  70.1 0.0 copy-done.1
  70.1 10.2 %depth.1 = bf16[1024,512]{1,0:T(8,128)(2,1)S(1)} custom-call(bf16[1024,512]{1,0:T(8,128)(2,1)S(1)} %bitcast.8, f32[4,512]{1,0:T(4,128)S(1)} %copy-done.3, bf16[3,512,1536]{2,1,0:T(8,128)(2,1)S(1)} %bitcast.5, bf16[3,512,512]{2,1,0:T(8,128)(2,1)S(1)} %copy-done, bf16[512,2048]{1,0:T(8,128)(2,1)S(1)} %copy-done.1, bf16[2048,512]{1,0:T(8,128)(2,1)S(1)} %copy-done.2), custom_call_target="tpu_custom_call" | custom-call | tf_op jit(solution)/shard_map/depth/pallas_call | solution.py:309
  80.3 35.6 %all_to_all.11 = bf16[128,8,512]{2,1,0:T(8,128)(2,1)S(1)} all-to-all(bf16[128,8,512]{2,1,0:T(8,128)(2,1)S(1)} %bitcast.9), channel_id=1, replica_groups={{0,16,32,48,6,22,38,54,12,28,44,60,2,18,34,50,8,24,40,56,14,30,46,62,4,..., dimensions={0} | all-to-all | bytes 2097152 | tf_op jit(solution)/shard_map/all_to_all | solution.py:319
  115.9 1.2 place.1
  (11 shorter events, 0.2 us)
Async XLA Ops:
  4.1 6.0 %collective-permute-start = (bf16[8,64,512]{2,1,0:T(8,128)(2,1)S(1)}, bf16[8,64,512]{2,1,0:T(8,128)(2,1)S(1)}, u32[]{:S(2)}, u32[]{:S(2)}) collective-permute-start(bf16[8,64,512]{2,1,0:T(8,128)(2,1)S(1)} %get-tuple-element.14), channel_id=1, source_target_pairs={{0,1},{1,0},{2,3},{3,2},{4,5},{5,4},{6,7},{7,6},{8,9},{9,8},{10,11... | collective-permute-start | bytes 1572872 | tf_op jit(solution)/shard_map/ppermute | solution.py:291
  7.4 33.0 %slice-start = ((s8[4718592]{0:T(1024)(128)(4,1)}), s8[4194304]{0:T(1024)(128)(4,1)S(1)}, s32[]{:S(2)}) async-start(s8[4718592]{0:T(1024)(128)(4,1)} %bitcast.4), calls=%async_computation.2 | async-start | bytes 8388608
  7.4 33.0 %slice-start.1 = ((s8[4718592]{0:T(1024)(128)(4,1)}), s8[524288]{0:T(1024)(128)(4,1)S(1)}, s32[]{:S(2)}) async-start(s8[4718592]{0:T(1024)(128)(4,1)} %bitcast.4), calls=%async_computation.3 | async-start | bytes 1048576
  10.0 30.4 %copy-start = (bf16[3,512,512]{2,1,0:T(8,128)(2,1)S(1)}, bf16[3,512,512]{2,1,0:T(8,128)(2,1)}, u32[]{:S(2)}) copy-start(bf16[3,512,512]{2,1,0:T(8,128)(2,1)} %out_ref.1) | copy-start | bytes 4718596
  10.0 30.4 %copy-start.3 = (f32[4,512]{1,0:T(4,128)S(1)}, f32[4,512]{1,0:T(4,128)}, u32[]{:S(2)}) copy-start(f32[4,512]{1,0:T(4,128)} %gain_ref.1) | copy-start | bytes 24580
  10.1 11.2 %collective-permute-start.1 = (bf16[2,64,512]{2,1,0:T(8,128)(2,1)S(1)}, bf16[2,64,512]{2,1,0:T(8,128)(2,1)S(1)}, u32[]{:S(2)}, u32[]{:S(2)}) collective-permute-start(bf16[2,64,512]{2,1,0:T(8,128)(2,1)S(1)} %pad_maximum_fusion.1), channel_id=1, source_target_pairs={{0,2},{2,4},{4,6},{6,8},{8,10},{10,12},{12,14},{14,0},{1,3},{3,5},... | collective-permute-start | bytes 393224 | tf_op jit(solution)/shard_map/ppermute | solution.py:295
  10.2 14.5 %collective-permute-start.2 = (bf16[2,64,512]{2,1,0:T(8,128)(2,1)S(1)}, bf16[2,64,512]{2,1,0:T(8,128)(2,1)S(1)}, u32[]{:S(2)}, u32[]{:S(2)}) collective-permute-start(bf16[2,64,512]{2,1,0:T(8,128)(2,1)S(1)} %pad_maximum_fusion.2), channel_id=1, source_target_pairs={{0,10},{2,12},{4,14},{6,0},{8,2},{10,4},{12,6},{14,8},{1,11},{3,13... | collective-permute-start | bytes 393224 | tf_op jit(solution)/shard_map/ppermute | solution.py:295
  15.8 13.8 %collective-permute-start.3 = (bf16[2,64,512]{2,1,0:T(8,128)(2,1)S(1)}, bf16[2,64,512]{2,1,0:T(8,128)(2,1)S(1)}, u32[]{:S(2)}, u32[]{:S(2)}) collective-permute-start(bf16[2,64,512]{2,1,0:T(8,128)(2,1)S(1)} %pad_maximum_fusion.3), channel_id=1, source_target_pairs={{0,6},{2,8},{4,10},{6,12},{8,14},{10,0},{12,2},{14,4},{1,7},{3,9},... | collective-permute-start | bytes 393224 | tf_op jit(solution)/shard_map/ppermute | solution.py:295
  15.9 14.0 %collective-permute-start.4 = (bf16[2,64,512]{2,1,0:T(8,128)(2,1)S(1)}, bf16[2,64,512]{2,1,0:T(8,128)(2,1)S(1)}, u32[]{:S(2)}, u32[]{:S(2)}) collective-permute-start(bf16[2,64,512]{2,1,0:T(8,128)(2,1)S(1)} %pad_maximum_fusion.4), channel_id=1, source_target_pairs={{0,8},{2,10},{4,12},{6,14},{8,0},{10,2},{12,4},{14,6},{1,9},{3,11}... | collective-permute-start | bytes 393224 | tf_op jit(solution)/shard_map/ppermute | solution.py:295
  19.7 17.0 %collective-permute-start.5 = (bf16[2,64,512]{2,1,0:T(8,128)(2,1)S(1)}, bf16[2,64,512]{2,1,0:T(8,128)(2,1)S(1)}, u32[]{:S(2)}, u32[]{:S(2)}) collective-permute-start(bf16[2,64,512]{2,1,0:T(8,128)(2,1)S(1)} %pad_maximum_fusion.5), channel_id=1, source_target_pairs={{0,12},{2,14},{4,0},{6,2},{8,4},{10,6},{12,8},{14,10},{1,13},{3,15... | collective-permute-start | bytes 393224 | tf_op jit(solution)/shard_map/ppermute | solution.py:295
  21.3 19.1 %collective-permute-start.6 = (bf16[2,64,512]{2,1,0:T(8,128)(2,1)S(1)}, bf16[2,64,512]{2,1,0:T(8,128)(2,1)S(1)}, u32[]{:S(2)}, u32[]{:S(2)}) collective-permute-start(bf16[2,64,512]{2,1,0:T(8,128)(2,1)S(1)} %pad_maximum_fusion.6), channel_id=1, source_target_pairs={{0,4},{2,6},{4,8},{6,10},{8,12},{10,14},{12,0},{14,2},{1,5},{3,7},... | collective-permute-start | bytes 393224 | tf_op jit(solution)/shard_map/ppermute | solution.py:295
  24.7 15.7 %collective-permute-start.7 = (bf16[2,64,512]{2,1,0:T(8,128)(2,1)S(1)}, bf16[2,64,512]{2,1,0:T(8,128)(2,1)S(1)}, u32[]{:S(2)}, u32[]{:S(2)}) collective-permute-start(bf16[2,64,512]{2,1,0:T(8,128)(2,1)S(1)} %pad_maximum_fusion.7), channel_id=1, source_target_pairs={{0,14},{2,0},{4,2},{6,4},{8,6},{10,8},{12,10},{14,12},{1,15},{3,1}... | collective-permute-start | bytes 393224 | tf_op jit(solution)/shard_map/ppermute | solution.py:295
  40.4 29.7 %copy-start.2 = (bf16[2048,512]{1,0:T(8,128)(2,1)S(1)}, bf16[2048,512]{1,0:T(8,128)(2,1)}, u32[]{:S(2)}) copy-start(bf16[2048,512]{1,0:T(8,128)(2,1)} %down_ref.1) | copy-start | bytes 6291460
  45.7 24.4 %copy-start.1 = (bf16[512,2048]{1,0:T(8,128)(2,1)S(1)}, bf16[512,2048]{1,0:T(8,128)(2,1)}, u32[]{:S(2)}) copy-start(bf16[512,2048]{1,0:T(8,128)(2,1)} %up_ref.1) | copy-start | bytes 6291460
